TPU v7x, 768 devices: a whole 4x8x12 slice. The times are simulated.
768 devices in a mesh: gx: 24 (over y_lo, z), gy: 8 (over y_hi, core), gz: 4 (over x).
Axes of the slice: x: 4, y: 8 (y_hi: 4, y_lo: 2; y = y_hi * 2 + y_lo), z: 12, core: 2. Of those that a mesh axis runs over, the one named last changes fastest.
Arguments:
- positions: float32 [48, 16, 8, 3, 16], P('gx', 'gy', 'gz'), may hold values from 0 to 5
- features: float32 [48, 16, 8, 16, 128], P('gx', 'gy', 'gz'), may hold values from -6 to 6
- species: int32 [48, 16, 8, 16], P('gx', 'gy', 'gz'), may hold values from 0 to 9
- counts: int32 [48, 16, 8], P('gx', 'gy', 'gz'), may hold values from 4 to 16
- species_energy: float32 [10], replicated, may hold values from -4 to 4
- radial_weight: float32 [8, 3, 128], replicated, may hold values from -2 to 2
- mix_weight: float32 [3, 128, 128], replicated, may hold values from -0.5 to 0.5
- readout: float32 [4, 128], replicated, may hold values from -0.5 to 0.5
Outputs:
- energies: float32 [48, 16, 8, 16], P('gx', 'gy', 'gz')
- forces: float32 [48, 16, 8, 3, 16], P('gx', 'gy', 'gz')
All inputs are finite; a program needn't handle non-finite values.
Results may differ from a plain program's by a relative error of at most 0.0003.
Values sent between devices are 32-bit elements; how exact they have to be, the bound alone decides.
A program may use at most 64 MiB of HBM per device.

v0:
```python
import math

import jax
import jax.numpy as jnp
import numpy as np
from jax import lax
from jax.sharding import PartitionSpec as P

CUTOFF = 5.0
CELL_SIDE = 5.0
SOFTENING = 0.5
DEGREE_OF = np.array([0, 1, 1, 1, 2, 2, 2, 2, 2])
NEIGHBOUR_SHIFTS = (
    np.array([[a, b, c] for a in (-1, 0, 1) for b in (-1, 0, 1) for c in (-1, 0, 1)]).T * CELL_SIDE
)


def with_halo(block, sides, width):
    for axis, dim in sides:
        count = lax.axis_size(axis)
        forward = [(i, i + 1) for i in range(count - 1)]
        forward.append((count - 1, 0))
        backward = [(target, source) for source, target in forward]
        low = lax.ppermute(
            lax.slice_in_dim(block, block.shape[dim] - width, None, axis=dim), axis, forward
        )
        high = lax.ppermute(lax.slice_in_dim(block, 0, width, axis=dim), axis, backward)
        block = jnp.concatenate([low, block, high], axis=dim)
    return block


def harmonics(direction):
    xpart, ypart, zpart = (direction[0], direction[1], direction[2])
    root_three = math.sqrt(3.0)
    root_fifteen = math.sqrt(15.0)
    root_five = math.sqrt(5.0)
    square = xpart * xpart + ypart * ypart + zpart * zpart
    return jnp.stack(
        [
            jnp.ones_like(xpart),
            root_three * xpart,
            root_three * ypart,
            root_three * zpart,
            root_fifteen * xpart * ypart,
            root_fifteen * ypart * zpart,
            0.5 * root_five * (3.0 * zpart * zpart - square),
            root_fifteen * xpart * zpart,
            0.5 * root_fifteen * (xpart * xpart - ypart * ypart),
        ]
    )


def cell_energy(ext_pos, ext_feat, corner, radial_weight, mix_weight, readout):
    slot_count = ext_pos.shape[-1]
    channels = ext_feat.shape[-1]
    basis_count = radial_weight.shape[0]
    highest = lax.Precision.HIGHEST
    anchor = jnp.zeros((), jnp.int32)
    block_pos = lax.dynamic_slice(
        ext_pos, (corner[0], corner[1], corner[2], anchor, anchor), (3, 3, 3, 3, slot_count)
    )
    block_feat = lax.dynamic_slice(
        ext_feat, (corner[0], corner[1], corner[2], anchor, anchor), (3, 3, 3, slot_count, channels)
    )
    own_pos = block_pos[1, 1, 1]
    offsets = jnp.asarray(NEIGHBOUR_SHIFTS, jnp.float32)
    near_pos = (
        jnp.transpose(block_pos.reshape(27, 3, slot_count), (1, 0, 2)) + offsets[:, :, None]
    ).reshape(3, 27 * slot_count)
    near_feat = block_feat.reshape(27 * slot_count, channels)
    relative = near_pos[:, None, :] - own_pos[:, :, None]
    distance = jnp.sqrt(jnp.sum(relative * relative, axis=0) + SOFTENING * SOFTENING)
    direction = relative / distance
    scaled = distance / CUTOFF
    envelope = jnp.where(
        scaled < 1.0, 1.0 - 21.0 * scaled**5 + 35.0 * scaled**6 - 15.0 * scaled**7, 0.0
    )
    column = lax.broadcasted_iota(jnp.int32, (slot_count, 27 * slot_count), 1)
    row_ids = lax.broadcasted_iota(jnp.int32, (slot_count, 27 * slot_count), 0)
    keep_pair = jnp.where(column == row_ids + 13 * slot_count, 0.0, 1.0)
    weighting = envelope * keep_pair * math.sqrt(2.0 / CUTOFF) / distance
    orders = jnp.arange(1, basis_count + 1).astype(jnp.float32)
    radial = jnp.sin(orders[:, None, None] * (math.pi / CUTOFF) * distance[None]) * weighting[None]
    harmonic = harmonics(direction)
    pair_tiles = radial[:, None] * harmonic[None]
    moments = jnp.einsum("nmik,kc->inmc", pair_tiles, near_feat, precision=highest)
    radial_wide = radial_weight[:, DEGREE_OF, :]
    summed = jnp.sum(moments * radial_wide[None], axis=1)
    scalar_inv = jnp.dot(summed[:, 0], mix_weight[0], precision=highest)
    vector_part = jnp.einsum("imc,cd->imd", summed[:, 1:4], mix_weight[1], precision=highest)
    tensor_part = jnp.einsum("imc,cd->imd", summed[:, 4:9], mix_weight[2], precision=highest)
    vector_inv = jnp.sum(vector_part * vector_part, axis=1)
    tensor_inv = jnp.sum(tensor_part * tensor_part, axis=1)
    return (
        jnp.dot(scalar_inv, readout[0], precision=highest)
        + jnp.dot(vector_inv, readout[1], precision=highest)
        + jnp.dot(tensor_inv, readout[2], precision=highest)
        + jnp.dot(scalar_inv * vector_inv, readout[3], precision=highest)
    )


def local_energies(
    ext_pos, ext_feat, cells_x, cells_y, cells_z, radial_weight, mix_weight, readout
):
    cell_count = cells_x * cells_y * cells_z
    cell_ids = jnp.arange(cell_count, dtype=jnp.int32)

    def one_cell(number):
        corner = jnp.stack(
            [number // (cells_y * cells_z), number // cells_z % cells_y, number % cells_z]
        )
        return cell_energy(ext_pos, ext_feat, corner, radial_weight, mix_weight, readout)

    result = lax.map(one_cell, cell_ids)
    return result.reshape(cells_x, cells_y, cells_z, ext_pos.shape[-1])


def fold_rims(field, axis_dim, inner):
    middle = lax.slice_in_dim(field, 2, 2 + inner, axis=axis_dim)
    lower = lax.slice_in_dim(field, 0, 1, axis=axis_dim)
    higher = lax.slice_in_dim(field, inner + 3, inner + 4, axis=axis_dim)
    widths_low = [(0, 0)] * field.ndim
    widths_high = [(0, 0)] * field.ndim
    widths_low[axis_dim] = (0, inner - 1)
    widths_high[axis_dim] = (inner - 1, 0)
    return middle + jnp.pad(lower, widths_low) + jnp.pad(higher, widths_high)


def per_device(
    positions, features, species, counts, species_energy, radial_weight, mix_weight, readout
):
    cells_x, cells_y, cells_z = (positions.shape[0], positions.shape[1], positions.shape[2])
    slot_count = positions.shape[-1]
    occupied = (
        jnp.arange(slot_count, dtype=jnp.int32)[None, None, None, :] < counts[..., None]
    ).astype(jnp.float32)
    masked = features * occupied[..., None]
    ext_pos, ext_feat = (
        with_halo(positions, (("gx", 0), ("gy", 1), ("gz", 2)), 1),
        with_halo(masked, (("gx", 0), ("gy", 1), ("gz", 2)), 1),
    )

    def energy_sum(pos_ext):
        layer = local_energies(
            pos_ext, ext_feat, cells_x, cells_y, cells_z, radial_weight, mix_weight, readout
        )
        return (jnp.sum(layer * occupied), layer)

    summed_energy, pullback, layer = jax.vjp(energy_sum, ext_pos, has_aux=True)
    (grad_ext,) = pullback(jnp.ones((), jnp.float32))
    returned = with_halo(grad_ext, (("gx", 0), ("gy", 1), ("gz", 2)), 1)
    gathered = fold_rims(fold_rims(fold_rims(returned, 0, cells_x), 1, cells_y), 2, cells_z)
    species_hot = (
        species[..., None] == jnp.arange(species_energy.shape[0], dtype=jnp.int32)
    ).astype(jnp.float32)
    table_part = jnp.sum(species_hot * species_energy, axis=-1)
    energies = occupied * (layer + table_part)
    return (energies, -gathered)


def solution(mesh):
    in_specs = (
        P("gx", "gy", "gz", None, None),
        P("gx", "gy", "gz", None, None),
        P("gx", "gy", "gz", None),
        P("gx", "gy", "gz"),
        P(),
        P(),
        P(),
        P(),
    )
    out_specs = (P("gx", "gy", "gz", None), P("gx", "gy", "gz", None, None))
    return jax.shard_map(
        per_device, mesh=mesh, in_specs=in_specs, out_specs=out_specs, check_vma=False
    )
```

profile of v0, /device:TPU:1, one launch (start us, length us, event | category | flops | bytes accessed | tf_op | source)
XLA Modules:
  0.0 391.1 jit_solution(3032698875846732686)
XLA Ops:
  2.4 4.8 %collective-permute-start = (f32[1,2,2,16,128]{4,3,2,1,0:T(8,128)S(1)}, f32[1,2,2,16,128]{4,3,2,1,0:T(8,128)S(1)}, u32[]{:S(2)}, u32[]{:S(2)}) collective-permute-start(f32[1,2,2,16,128]{4,3,2,1,0:T(8,128)S(1)} %get-tuple-element.2884), channel_id=1, source_target_pairs={{0,32},{32,64},{64,96},{96,128},{128,160},{160,192},{192,224},{224... | collective-permute-start | bytes 98312 | tf_op jit(solution)/shard_map/ppermute | solution.py:24
  7.2 13.2 %collective-permute-start.1 = (f32[1,2,2,16,128]{4,3,2,1,0:T(8,128)S(1)}, f32[1,2,2,16,128]{4,3,2,1,0:T(8,128)S(1)}, u32[]{:S(2)}, u32[]{:S(2)}) collective-permute-start(f32[1,2,2,16,128]{4,3,2,1,0:T(8,128)S(1)} %get-tuple-element.2885), channel_id=1, source_target_pairs={{32,0},{64,32},{96,64},{128,96},{160,128},{192,160},{224,192},{256... | collective-permute-start | bytes 98312 | tf_op jit(solution)/shard_map/ppermute | solution.py:27
  21.2 1.9 collective-permute-start.6
  23.1 5.5 %collective-permute-start.7 = (f32[1,2,2,3,16]{4,3,2,1,0:T(4,128)S(1)}, f32[1,2,2,3,16]{4,3,2,1,0:T(4,128)S(1)}, u32[]{:S(2)}, u32[]{:S(2)}) collective-permute-start(f32[1,2,2,3,16]{4,3,2,1,0:T(4,128)S(1)} %copy.71), channel_id=1, source_target_pairs={{32,0},{64,32},{96,64},{128,96},{160,128},{192,160},{224,192},{256... | collective-permute-start | bytes 2312 | tf_op jit(solution)/shard_map/ppermute | solution.py:27
  31.9 5.6 %collective-permute-start.8 = (f32[4,1,2,3,16]{4,3,2,1,0:T(4,128)S(1)}, f32[4,1,2,3,16]{4,3,2,1,0:T(4,128)S(1)}, u32[]{:S(2)}, u32[]{:S(2)}) collective-permute-start(f32[4,1,2,3,16]{4,3,2,1,0:T(4,128)S(1)} %get-tuple-element.2886), channel_id=1, source_target_pairs={{0,4},{4,8},{8,12},{12,16},{16,20},{20,24},{24,28},{28,0},{1,5},{5... | collective-permute-start | bytes 4616 | tf_op jit(solution)/shard_map/ppermute | solution.py:24
  37.5 1.9 collective-permute-start.9
  40.1 3.4 collective-permute-done.9
  43.6 1.9 collective-permute-start.2
  45.6 2.4 collective-permute-start.3
  48.0 3.1 collective-permute-start.10
  51.1 3.4 collective-permute-start.11
  54.6 2.2 collective-permute-start.4
  56.8 4.3 %collective-permute-start.5 = (f32[4,4,1,16,128]{4,3,2,1,0:T(8,128)S(1)}, f32[4,4,1,16,128]{4,3,2,1,0:T(8,128)S(1)}, u32[]{:S(2)}, u32[]{:S(2)}) collective-permute-start(f32[4,4,1,16,128]{4,3,2,1,0:T(8,128)S(1)} %get-tuple-element.2870), channel_id=1, source_target_pairs={{1,0},{2,1},{3,2},{0,3},{5,4},{6,5},{7,6},{4,7},{9,8},{10,9},{11,1... | collective-permute-start | bytes 393224 | tf_op jit(solution)/shard_map/ppermute | solution.py:27
  63.1 139.8 %while.96 = (s32[]{:T(128)}, f32[8,16]{1,0:T(8,128)S(1)}, s32[8]{0:T(128)S(1)}, s32[8]{0:T(128)S(1)}, s32[8]{0:T(128)S(1)}, /*index=5*/f32[8,3,16,432]{3,2,1,0:T...) while((s32[]{:T(128)}, f32[8,16]{1,0:T(8,128)S(1)}, ...), condition=%wide.region_5.6_spmd.clone.clone, body=%wide.region_0.5_spmd.clone.clone.sunk | while | flops 794692416 | bytes 5803510 | solution.py:114
  69.5 2.1 fusion.223
  74.6 1.8 fusion.230
  76.4 1.6 multiply_dynamic-update-slice_fusion.28
  87.0 2.1 fusion.223
  92.1 1.8 fusion.230
  104.5 2.1 fusion.223
  109.6 1.8 fusion.230
  122.0 2.1 fusion.223
  127.1 1.8 fusion.230
  139.4 2.1 fusion.223
  144.5 1.8 fusion.230
  156.9 2.1 fusion.223
  161.9 1.8 fusion.230
  163.7 1.6 multiply_dynamic-update-slice_fusion.28
  174.4 2.1 fusion.223
  179.4 1.8 fusion.230
  191.8 2.1 fusion.223
  196.9 1.8 fusion.230
  202.9 155.1 %while.95 = (s32[]{:T(128)}, f32[4,4,4,3,16]{4,2,3,1,0:T(4,128)S(1)}, s32[8]{0:T(128)S(1)}, s32[8]{0:T(128)S(1)}, s32[8]{0:T(128)S(1)}, /*index=5*/f32[8,16,432]...) while((s32[]{:T(128)}, ...), condition=%wide.region_15.16_spmd.clone, body=%wide.region_7.15_spmd.clone.sunk | while | flops 795890944 | bytes 5258429 | solution.py:114
  207.9 3.3 multiply_reduce_fusion.7
  218.0 2.0 copy_add_fusion.2
  220.1 2.2 add_any.520
  227.3 3.3 multiply_reduce_fusion.7
  237.4 2.0 copy_add_fusion.2
  239.5 2.2 add_any.520
  246.7 3.3 multiply_reduce_fusion.7
  256.8 2.0 copy_add_fusion.2
  258.9 2.2 add_any.520
  266.1 3.3 multiply_reduce_fusion.7
  276.2 2.0 copy_add_fusion.2
  278.2 2.2 add_any.520
  285.5 3.3 multiply_reduce_fusion.7
  295.6 2.0 copy_add_fusion.2
  297.6 2.2 add_any.520
  304.9 3.3 multiply_reduce_fusion.7
  315.0 2.0 copy_add_fusion.2
  317.0 2.2 add_any.520
  324.3 3.3 multiply_reduce_fusion.7
  334.3 2.0 copy_add_fusion.2
  336.4 2.2 add_any.520
  343.6 3.3 multiply_reduce_fusion.7
  353.7 2.0 copy_add_fusion.2
  355.8 2.2 add_any.520
  358.0 1.9 collective-permute-start.12
  360.0 5.5 %collective-permute-start.13 = (f32[1,4,4,3,16]{4,2,3,1,0:T(4,128)S(1)}, f32[1,4,4,3,16]{4,2,3,1,0:T(4,128)S(1)}, u32[]{:S(2)}, u32[]{:S(2)}) collective-permute-start(f32[1,4,4,3,16]{4,2,3,1,0:T(4,128)S(1)} %get-tuple-element.2880), channel_id=1, source_target_pairs={{32,0},{64,32},{96,64},{128,96},{160,128},{192,160},{224,192},{256... | collective-permute-start | bytes 9224 | tf_op jit(solution)/shard_map/ppermute | solution.py:27
  366.4 8.5 %collective-permute-start.14 = (f32[6,1,4,3,16]{4,2,3,1,0:T(4,128)S(1)}, f32[6,1,4,3,16]{4,2,3,1,0:T(4,128)S(1)}, u32[]{:S(2)}, u32[]{:S(2)}) collective-permute-start(f32[6,1,4,3,16]{4,2,3,1,0:T(4,128)S(1)} %get-tuple-element.2876), channel_id=1, source_target_pairs={{0,4},{4,8},{8,12},{12,16},{16,20},{20,24},{24,28},{28,0},{1,5},{5... | collective-permute-start | bytes 13832 | tf_op jit(solution)/shard_map/ppermute | solution.py:24
  374.9 1.9 collective-permute-start.15
  376.9 4.2 %collective-permute-done.15 = f32[6,1,4,3,16]{4,2,3,1,0:T(4,128)S(1)} collective-permute-done((f32[6,1,4,3,16]{4,2,3,1,0:T(4,128)S(1)}, f32[6,1,4,3,16]{4,2,3,1,0:T(4,128)S(1)}, u32[]{:S(2)}, u32[]{:S(2)}) %collective-permute-start.15) | collective-permute-done | bytes 4640 | tf_op jit(solution)/shard_map/ppermute | solution.py:27
  381.2 2.7 collective-permute-start.16
  383.9 4.6 %collective-permute-start.17 = (f32[6,6,1,3,16]{4,2,3,1,0:T(1,128)S(1)}, f32[6,6,1,3,16]{4,2,3,1,0:T(1,128)S(1)}, u32[]{:S(2)}, u32[]{:S(2)}) collective-permute-start(f32[6,6,1,3,16]{4,2,3,1,0:T(1,128)S(1)} %get-tuple-element.2872), channel_id=1, source_target_pairs={{1,0},{2,1},{3,2},{0,3},{5,4},{6,5},{7,6},{4,7},{9,8},{10,9},{11,1... | collective-permute-start | bytes 20744 | tf_op jit(solution)/shard_map/ppermute | solution.py:27
  (619 shorter events, 186.9 us)
Async XLA Ops:
  0.6 60.8 %copy-start = (f32[8,3,128]{2,0,1:T(8,128)S(1)}, f32[8,3,128]{2,0,1:T(8,128)}, u32[]{:S(2)}) copy-start(f32[8,3,128]{2,0,1:T(8,128)} %param.20) | copy-start | bytes 36868
  2.3 60.8 %copy-start.1 = (f32[3,27]{1,0:T(4,128)S(1)}, f32[3,27]{1,0:T(4,128)}, u32[]{:S(2)}) copy-start(f32[3,27]{1,0:T(4,128)} %constant.816) | copy-start | bytes 976
  2.4 41.2 %collective-permute-start = (f32[1,2,2,16,128]{4,3,2,1,0:T(8,128)S(1)}, f32[1,2,2,16,128]{4,3,2,1,0:T(8,128)S(1)}, u32[]{:S(2)}, u32[]{:S(2)}) collective-permute-start(f32[1,2,2,16,128]{4,3,2,1,0:T(8,128)S(1)} %get-tuple-element.2884), channel_id=1, source_target_pairs={{0,32},{32,64},{64,96},{96,128},{128,160},{160,192},{192,224},{224... | collective-permute-start | bytes 98312 | tf_op jit(solution)/shard_map/ppermute | solution.py:24
  7.2 36.4 %collective-permute-start.1 = (f32[1,2,2,16,128]{4,3,2,1,0:T(8,128)S(1)}, f32[1,2,2,16,128]{4,3,2,1,0:T(8,128)S(1)}, u32[]{:S(2)}, u32[]{:S(2)}) collective-permute-start(f32[1,2,2,16,128]{4,3,2,1,0:T(8,128)S(1)} %get-tuple-element.2885), channel_id=1, source_target_pairs={{32,0},{64,32},{96,64},{128,96},{160,128},{192,160},{224,192},{256... | collective-permute-start | bytes 98312 | tf_op jit(solution)/shard_map/ppermute | solution.py:27
  21.2 10.0 %collective-permute-start.6 = (f32[1,2,2,3,16]{4,3,2,1,0:T(4,128)S(1)}, f32[1,2,2,3,16]{4,3,2,1,0:T(4,128)S(1)}, u32[]{:S(2)}, u32[]{:S(2)}) collective-permute-start(f32[1,2,2,3,16]{4,3,2,1,0:T(4,128)S(1)} %copy.70), channel_id=1, source_target_pairs={{0,32},{32,64},{64,96},{96,128},{128,160},{160,192},{192,224},{224... | collective-permute-start | bytes 2312 | tf_op jit(solution)/shard_map/ppermute | solution.py:24
  23.1 8.8 %collective-permute-start.7 = (f32[1,2,2,3,16]{4,3,2,1,0:T(4,128)S(1)}, f32[1,2,2,3,16]{4,3,2,1,0:T(4,128)S(1)}, u32[]{:S(2)}, u32[]{:S(2)}) collective-permute-start(f32[1,2,2,3,16]{4,3,2,1,0:T(4,128)S(1)} %copy.71), channel_id=1, source_target_pairs={{32,0},{64,32},{96,64},{128,96},{160,128},{192,160},{224,192},{256... | collective-permute-start | bytes 2312 | tf_op jit(solution)/shard_map/ppermute | solution.py:27
  31.9 8.2 %collective-permute-start.8 = (f32[4,1,2,3,16]{4,3,2,1,0:T(4,128)S(1)}, f32[4,1,2,3,16]{4,3,2,1,0:T(4,128)S(1)}, u32[]{:S(2)}, u32[]{:S(2)}) collective-permute-start(f32[4,1,2,3,16]{4,3,2,1,0:T(4,128)S(1)} %get-tuple-element.2886), channel_id=1, source_target_pairs={{0,4},{4,8},{8,12},{12,16},{16,20},{20,24},{24,28},{28,0},{1,5},{5... | collective-permute-start | bytes 4616 | tf_op jit(solution)/shard_map/ppermute | solution.py:24
  37.5 6.0 %collective-permute-start.9 = (f32[4,1,2,3,16]{4,3,2,1,0:T(4,128)S(1)}, f32[4,1,2,3,16]{4,3,2,1,0:T(4,128)S(1)}, u32[]{:S(2)}, u32[]{:S(2)}) collective-permute-start(f32[4,1,2,3,16]{4,3,2,1,0:T(4,128)S(1)} %get-tuple-element.2887), channel_id=1, source_target_pairs={{4,0},{8,4},{12,8},{16,12},{20,16},{24,20},{28,24},{0,28},{5,1},{9... | collective-permute-start | bytes 4616 | tf_op jit(solution)/shard_map/ppermute | solution.py:27
  43.6 10.9 %collective-permute-start.2 = (f32[4,1,2,16,128]{4,3,2,1,0:T(8,128)S(1)}, f32[4,1,2,16,128]{4,3,2,1,0:T(8,128)S(1)}, u32[]{:S(2)}, u32[]{:S(2)}) collective-permute-start(f32[4,1,2,16,128]{4,3,2,1,0:T(8,128)S(1)} %get-tuple-element.2878), channel_id=1, source_target_pairs={{0,4},{4,8},{8,12},{12,16},{16,20},{20,24},{24,28},{28,0},{1,5},{5... | collective-permute-start | bytes 196616 | tf_op jit(solution)/shard_map/ppermute | solution.py:24
  45.6 9.0 %collective-permute-start.3 = (f32[4,1,2,16,128]{4,3,2,1,0:T(8,128)S(1)}, f32[4,1,2,16,128]{4,3,2,1,0:T(8,128)S(1)}, u32[]{:S(2)}, u32[]{:S(2)}) collective-permute-start(f32[4,1,2,16,128]{4,3,2,1,0:T(8,128)S(1)} %get-tuple-element.2879), channel_id=1, source_target_pairs={{4,0},{8,4},{12,8},{16,12},{20,16},{24,20},{28,24},{0,28},{5,1},{9... | collective-permute-start | bytes 196616 | tf_op jit(solution)/shard_map/ppermute | solution.py:27
  48.0 14.0 %collective-permute-start.10 = (f32[4,4,1,3,16]{4,3,2,1,0:T(4,128)S(1)}, f32[4,4,1,3,16]{4,3,2,1,0:T(4,128)S(1)}, u32[]{:S(2)}, u32[]{:S(2)}) collective-permute-start(f32[4,4,1,3,16]{4,3,2,1,0:T(4,128)S(1)} %get-tuple-element.2882), channel_id=1, source_target_pairs={{0,1},{1,2},{2,3},{3,0},{4,5},{5,6},{6,7},{7,4},{8,9},{9,10},{10,1... | collective-permute-start | bytes 9224 | tf_op jit(solution)/shard_map/ppermute | solution.py:24
  51.1 10.9 %collective-permute-start.11 = (f32[4,4,1,3,16]{4,3,2,1,0:T(4,128)S(1)}, f32[4,4,1,3,16]{4,3,2,1,0:T(4,128)S(1)}, u32[]{:S(2)}, u32[]{:S(2)}) collective-permute-start(f32[4,4,1,3,16]{4,3,2,1,0:T(4,128)S(1)} %get-tuple-element.2883), channel_id=1, source_target_pairs={{1,0},{2,1},{3,2},{0,3},{5,4},{6,5},{7,6},{4,7},{9,8},{10,9},{11,1... | collective-permute-start | bytes 9224 | tf_op jit(solution)/shard_map/ppermute | solution.py:27
  54.6 7.5 %collective-permute-start.4 = (f32[4,4,1,16,128]{4,3,2,1,0:T(8,128)S(1)}, f32[4,4,1,16,128]{4,3,2,1,0:T(8,128)S(1)}, u32[]{:S(2)}, u32[]{:S(2)}) collective-permute-start(f32[4,4,1,16,128]{4,3,2,1,0:T(8,128)S(1)} %get-tuple-element.2869), channel_id=1, source_target_pairs={{0,1},{1,2},{2,3},{3,0},{4,5},{5,6},{6,7},{7,4},{8,9},{9,10},{10,1... | collective-permute-start | bytes 393224 | tf_op jit(solution)/shard_map/ppermute | solution.py:24
  56.8 6.3 %collective-permute-start.5 = (f32[4,4,1,16,128]{4,3,2,1,0:T(8,128)S(1)}, f32[4,4,1,16,128]{4,3,2,1,0:T(8,128)S(1)}, u32[]{:S(2)}, u32[]{:S(2)}) collective-permute-start(f32[4,4,1,16,128]{4,3,2,1,0:T(8,128)S(1)} %get-tuple-element.2870), channel_id=1, source_target_pairs={{1,0},{2,1},{3,2},{0,3},{5,4},{6,5},{7,6},{4,7},{9,8},{10,9},{11,1... | collective-permute-start | bytes 393224 | tf_op jit(solution)/shard_map/ppermute | solution.py:27
  202.9 173.9 %copy-start.4 = (s32[2,2,2,16]{3,2,1,0:T(2,128)S(1)}, s32[2,2,2,16]{3,2,1,0:T(2,128)}, u32[]{:S(2)}) copy-start(s32[2,2,2,16]{3,2,1,0:T(2,128)} %param.17) | copy-start | bytes 1540
  202.9 173.9 %copy-start.5 = (f32[10]{0:T(128)S(1)}, f32[10]{0:T(128)}, u32[]{:S(2)}) copy-start(f32[10]{0:T(128)} %param.19) | copy-start | bytes 124
  202.9 185.6 %copy-start.2 = (s32[2,2,2]{2,1,0:T(2,128)S(1)}, s32[2,2,2]{2,1,0:T(2,128)}, u32[]{:S(2)}) copy-start(s32[2,2,2]{2,1,0:T(2,128)} %param.18) | copy-start | bytes 100
  202.9 187.3 %copy-start.3 = (pred[2]{0:T(512)(128)(4,1)S(1)}, pred[2]{0:T(512)(128)(4,1)}, u32[]{:S(2)}) copy-start(pred[2]{0:T(512)(128)(4,1)} %constant.531.clone.1) | copy-start | bytes 10
  358.0 7.4 %collective-permute-start.12 = (f32[1,4,4,3,16]{4,2,3,1,0:T(4,128)S(1)}, f32[1,4,4,3,16]{4,2,3,1,0:T(4,128)S(1)}, u32[]{:S(2)}, u32[]{:S(2)}) collective-permute-start(f32[1,4,4,3,16]{4,2,3,1,0:T(4,128)S(1)} %get-tuple-element.2881), channel_id=1, source_target_pairs={{0,32},{32,64},{64,96},{96,128},{128,160},{160,192},{192,224},{224... | collective-permute-start | bytes 9224 | tf_op jit(solution)/shard_map/ppermute | solution.py:24
  360.0 6.4 %collective-permute-start.13 = (f32[1,4,4,3,16]{4,2,3,1,0:T(4,128)S(1)}, f32[1,4,4,3,16]{4,2,3,1,0:T(4,128)S(1)}, u32[]{:S(2)}, u32[]{:S(2)}) collective-permute-start(f32[1,4,4,3,16]{4,2,3,1,0:T(4,128)S(1)} %get-tuple-element.2880), channel_id=1, source_target_pairs={{32,0},{64,32},{96,64},{128,96},{160,128},{192,160},{224,192},{256... | collective-permute-start | bytes 9224 | tf_op jit(solution)/shard_map/ppermute | solution.py:27
  366.4 10.5 %collective-permute-start.14 = (f32[6,1,4,3,16]{4,2,3,1,0:T(4,128)S(1)}, f32[6,1,4,3,16]{4,2,3,1,0:T(4,128)S(1)}, u32[]{:S(2)}, u32[]{:S(2)}) collective-permute-start(f32[6,1,4,3,16]{4,2,3,1,0:T(4,128)S(1)} %get-tuple-element.2876), channel_id=1, source_target_pairs={{0,4},{4,8},{8,12},{12,16},{16,20},{20,24},{24,28},{28,0},{1,5},{5... | collective-permute-start | bytes 13832 | tf_op jit(solution)/shard_map/ppermute | solution.py:24
  374.9 6.3 %collective-permute-start.15 = (f32[6,1,4,3,16]{4,2,3,1,0:T(4,128)S(1)}, f32[6,1,4,3,16]{4,2,3,1,0:T(4,128)S(1)}, u32[]{:S(2)}, u32[]{:S(2)}) collective-permute-start(f32[6,1,4,3,16]{4,2,3,1,0:T(4,128)S(1)} %get-tuple-element.2877), channel_id=1, source_target_pairs={{4,0},{8,4},{12,8},{16,12},{20,16},{24,20},{28,24},{0,28},{5,1},{9... | collective-permute-start | bytes 13832 | tf_op jit(solution)/shard_map/ppermute | solution.py:27
  381.2 7.9 %collective-permute-start.16 = (f32[6,6,1,3,16]{4,2,3,1,0:T(1,128)S(1)}, f32[6,6,1,3,16]{4,2,3,1,0:T(1,128)S(1)}, u32[]{:S(2)}, u32[]{:S(2)}) collective-permute-start(f32[6,6,1,3,16]{4,2,3,1,0:T(1,128)S(1)} %get-tuple-element.2871), channel_id=1, source_target_pairs={{0,1},{1,2},{2,3},{3,0},{4,5},{5,6},{6,7},{7,4},{8,9},{9,10},{10,1... | collective-permute-start | bytes 20744 | tf_op jit(solution)/shard_map/ppermute | solution.py:24
  383.9 6.1 %collective-permute-start.17 = (f32[6,6,1,3,16]{4,2,3,1,0:T(1,128)S(1)}, f32[6,6,1,3,16]{4,2,3,1,0:T(1,128)S(1)}, u32[]{:S(2)}, u32[]{:S(2)}) collective-permute-start(f32[6,6,1,3,16]{4,2,3,1,0:T(1,128)S(1)} %get-tuple-element.2872), channel_id=1, source_target_pairs={{1,0},{2,1},{3,2},{0,3},{5,4},{6,5},{7,6},{4,7},{9,8},{10,9},{11,1... | collective-permute-start | bytes 20744 | tf_op jit(solution)/shard_map/ppermute | solution.py:27
where the time goes:
time: 399 us; the launch traced here: 391 us
  other arithmetic  107 us (27%)
  local copies, waits for them, and re-layouts  97.8 us (25%)
  starting transfers between devices  75.3 us (19%)
  matrix products  74.6 us (19%)
  loops' own time  24.7 us (6%)
  waiting for transfers between devices  10.3 us (3%)
    dynamic_update_slice x56, other arithmetic, local_energies(): result = lax.map(one_cell, cell_ids)  44.7 us
    dot_general x16, matrix products, cell_energy(): jnp.einsum('nmik,kc->inmc', pair_tiles, near_feat, precision=highest)  43.4 us
    ppermute x9, starting transfers between devices, with_halo(): lax.ppermute(lax.slice_in_dim(block, 0, width, axis=dim), axis, backward)  42.7 us
    ppermute x9, starting transfers between devices, with_halo(): lax.ppermute(lax.slice_in_dim(block, block.shape[dim] - width, None, axis...  32.6 us
    another operation x2, loops' own time, local_energies(): result = lax.map(one_cell, cell_ids)  24.7 us
    dynamic_update_slice x72, local copies, waits for them, and re-layouts, local_energies(): result = lax.map(one_cell, cell_ids)  24.2 us
    dynamic_slice x32, local copies, waits for them, and re-layouts, local_energies(): result = lax.map(one_cell, cell_ids)  20.5 us
    add_any x16, local copies, waits for them, and re-layouts, cell_energy(): lax.dynamic_slice(ext_pos, (corner[0], corner[1], corner[2], anchor, anch...  18 us
  transfers between devices with their start and end apart: 18, of which 5 were waited for; matrix products, arithmetic and copies ran while one was open for 2% of the time, Pallas kernels for 0%

commit v1 on v0

v1 whole, which is shorter than its diff:
```python
import math

import jax
import jax.numpy as jnp
import numpy as np
from jax import lax
from jax.experimental import pallas as pl
from jax.experimental.pallas import tpu as pltpu
from jax.sharding import PartitionSpec as P

CUTOFF = 5.0
CELL_SIDE = 5.0
SOFTENING = 0.5
BASIS = 8
SLOTS = 16
LANES = 128
CHUNKS = 4
NEAR = CHUNKS * LANES
ROWS = BASIS * 9 * SLOTS
DEGREE_OF = (0, 1, 1, 1, 2, 2, 2, 2, 2)
SELF = 13
MESH = pl.DeviceIdType.MESH
AXES = ("gx", "gy", "gz")
R3, R5, R15 = math.sqrt(3.0), math.sqrt(5.0), math.sqrt(15.0)
F32, BF16 = jnp.float32, jnp.bfloat16

OFFSETS = [(a, b, c) for a in (-1, 0, 1) for b in (-1, 0, 1) for c in (-1, 0, 1)]
CELLS = [(x, y, z) for x in (0, 1) for y in (0, 1) for z in (0, 1)]


def near_table(cell):
    sign = [1 if c == 1 else -1 for c in cell]
    rim = [0 if s == 1 else 1 for s in sign]
    taken = {(0, q) for q in range(8)}
    table = [(0, q, SELF, q) for q in range(8)]
    late = []
    for size in (1, 2, 3):
        for subset in range(1, 8):
            dims = [d for d in range(3) if subset >> d & 1]
            if len(dims) != size:
                continue
            off = [sign[d] if d in dims else 0 for d in range(3)]
            domain = OFFSETS.index(tuple(off))
            for q, coords in enumerate(CELLS):
                if any(coords[d] != rim[d] for d in dims):
                    continue
                for chunk in range(1, CHUNKS):
                    if (chunk, q) not in taken:
                        taken.add((chunk, q))
                        table.append((chunk, q, domain, q))
                        break
                else:
                    late.append((domain, q))
    for domain, q in late:
        chunk, place = min(
            (c, p) for c in range(1, CHUNKS) for p in range(8) if (c, p) not in taken
        )
        taken.add((chunk, place))
        table.append((chunk, place, domain, q))
    return table


TABLES = [near_table(cell) for cell in CELLS]


def grouped(table, chunk):
    groups = {}
    for c, place, domain, q in table:
        if c == chunk:
            groups.setdefault((domain, (place - q) % 8), []).append(place)
    return sorted(groups.items())


def places_mask(places):
    lane = lax.broadcasted_iota(jnp.int32, (8, LANES), 1)
    mask = None
    for place in places:
        one = (lane >= place * SLOTS) & (lane < (place + 1) * SLOTS)
        mask = one if mask is None else mask | one
    return mask


def neighbour(domain):
    place = []
    for axis, step in zip(AXES, OFFSETS[domain]):
        count = lax.axis_size(axis)
        place.append(lax.rem(lax.axis_index(axis) + step + count, count))
    return tuple(place)


def rim_of(domain):
    return tuple(
        pl.ds(0, 2) if step == 0 else pl.ds(1 if step == 1 else 0, 1) for step in OFFSETS[domain]
    )


def greet():
    barrier = pltpu.get_barrier_semaphore()
    for domain in range(27):
        if domain != SELF:
            pl.semaphore_signal(
                barrier, inc=1, device_id=neighbour(domain), device_id_type=MESH
            )
    return barrier


def halo_kernel(pos_ref, feat_ref, counts_ref, tiles_ref, feats_ref, tile, masked, sends, recvs, own):
    barrier = greet()
    slot = lax.broadcasted_iota(jnp.int32, (SLOTS, LANES), 0)
    tile[...] = jnp.zeros_like(tile)
    for q, (x, y, z) in enumerate(CELLS):
        tile[0:3, q * SLOTS : (q + 1) * SLOTS] = pos_ref[x, y, :, z, :]
        masked[x, y, z] = jnp.where(slot < counts_ref[x, y, z], feat_ref[x, y, z], 0.0)
    lane = lax.broadcasted_iota(jnp.int32, (8, LANES), 1)
    row = lax.broadcasted_iota(jnp.int32, (8, LANES), 0)
    shift = jnp.where(row == 0, lane // 64, jnp.where(row == 1, lane // 32 % 2, lane // 16 % 2))
    tile[...] = tile[...] + CELL_SIDE * shift.astype(F32)
    pl.semaphore_wait(barrier, 26)
    mine = [
        pltpu.make_async_copy(tile, tiles_ref.at[SELF], own.at[0]),
        pltpu.make_async_copy(masked, feats_ref.at[SELF], own.at[1]),
    ]
    copies = []
    for domain in range(27):
        if domain == SELF:
            continue
        there, rim, back = neighbour(domain), rim_of(domain), 26 - domain
        copies.append(
            pltpu.make_async_remote_copy(
                tile, tiles_ref.at[back], sends.at[0, domain], recvs.at[0, back],
                device_id=there, device_id_type=MESH,
            )
        )
        copies.append(
            pltpu.make_async_remote_copy(
                masked.at[rim], feats_ref.at[(back,) + rim], sends.at[1, domain],
                recvs.at[1, back], device_id=there, device_id_type=MESH,
            )
        )
    for copy in copies:
        copy.start()
    for copy in mine:
        copy.start()
    for copy in mine:
        copy.wait()
    for copy in copies:
        copy.wait()


def halves(value):
    high = value.astype(BF16)
    return high, (value - high.astype(F32)).astype(BF16)


def dot(a, b, rhs_dim=0):
    return lax.dot_general(
        a, b, (((1,), (rhs_dim,)), ((), ())), preferred_element_type=F32
    )


def dot_split(a, b, rhs_dim=0):
    a_high, a_low = halves(a)
    b_high, b_low = halves(b)
    return (
        dot(a_low, b_high, rhs_dim) + dot(a_high, b_low, rhs_dim) + dot(a_high, b_high, rhs_dim)
    )


def harmonics(ux, uy, uz):
    square = ux * ux + uy * uy + uz * uz
    return [
        None,
        R3 * ux,
        R3 * uy,
        R3 * uz,
        R15 * ux * uy,
        R15 * uy * uz,
        0.5 * R5 * (3.0 * uz * uz - square),
        R15 * ux * uz,
        0.5 * R15 * (ux * ux - uy * uy),
    ]


def radial_parts(distance, inverse, keep):
    t = jnp.minimum(distance * (1.0 / CUTOFF), 1.0)
    phi = math.pi * (t - 0.5)
    sq = phi * phi
    sine, cosine = 0.0, 0.0
    for k in range(6, -1, -1):
        if k < 6:
            sine = sine * sq + (-1) ** k / math.factorial(2 * k + 1)
        cosine = cosine * sq + (-1) ** k / math.factorial(2 * k)
    s1, c1 = cosine, -(sine * phi)
    t2 = t * t
    t4 = t2 * t2
    env = jnp.where(keep, 1.0 + t4 * t * (-21.0 + t * (35.0 - 15.0 * t)), 0.0)
    gap = 1.0 - t
    env_d = jnp.where(keep, (-105.0 / CUTOFF) * t4 * gap * gap, 0.0)
    scale = math.sqrt(2.0 / CUTOFF)
    w = scale * env * inverse
    w_d = inverse * (scale * env_d - w)
    twice = 2.0 * c1
    sines, cosines = [s1], [c1]
    for n in range(1, BASIS):
        sines.append(twice * sines[-1] - (sines[-2] if n > 1 else 0.0))
        cosines.append(twice * cosines[-1] - (cosines[-2] if n > 1 else 1.0))
    values = [s * w for s in sines]
    slopes = [
        ((n + 1) * math.pi / CUTOFF) * (c * w) + s * w_d
        for n, (s, c) in enumerate(zip(sines, cosines))
    ]
    return values, slopes


def force_kernel(
    tiles_ref, feats_ref, species_ref, counts_ref, table_ref, radial_ref, mix_ref, readout_ref,
    energy_ref, grads_ref,
    npos, post, fcat, fback, pair, mom, summed, rad, geo, gpair, dpair, ngrad, center,
):
    row = lax.broadcasted_iota(jnp.int32, (8, LANES), 0)
    for s in range(8):
        for chunk in range(CHUNKS):
            value = jnp.full((8, LANES), 100.0, F32)
            for (domain, turn), places in grouped(TABLES[s], chunk):
                ox, oy, oz = (2.0 * CELL_SIDE * o for o in OFFSETS[domain])
                piece = tiles_ref[domain]
                if domain != SELF:
                    piece = piece + jnp.where(row == 0, ox, jnp.where(row == 1, oy, oz))
                if turn:
                    piece = pltpu.roll(piece, turn * SLOTS, 1)
                value = piece if len(places) == 8 else jnp.where(places_mask(places), piece, value)
            npos[s, :, chunk * LANES : (chunk + 1) * LANES] = value
        filled = {(c, p): (domain, q) for c, p, domain, q in TABLES[s]}
        for chunk in range(CHUNKS):
            for place in range(8):
                at = slice(chunk * LANES + place * SLOTS, chunk * LANES + (place + 1) * SLOTS)
                low_at = slice(NEAR + at.start, NEAR + at.stop)
                if (chunk, place) in filled:
                    domain, q = filled[(chunk, place)]
                    high, low = halves(feats_ref[domain * 8 + q])
                else:
                    high = low = jnp.zeros((SLOTS, LANES), BF16)
                fcat[s, at, 0:128] = high
                fcat[s, at, 128:256] = low
                fcat[s, low_at, 0:128] = high
                fcat[s, low_at, 128:256] = jnp.zeros((SLOTS, LANES), BF16)
                fback[s, at, 0:128] = high
                fback[s, at, 128:256] = high
                fback[s, at, 256:384] = low
    mine = tiles_ref[SELF]
    post[...] = jnp.transpose(jnp.concatenate([mine] * 16, axis=0))
    ngrad[...] = jnp.zeros_like(ngrad)

    def forward(s, carry):
        own = pl.ds(pl.multiple_of(s * SLOTS, SLOTS), SLOTS)
        for chunk in range(CHUNKS):
            at = slice(chunk * LANES, (chunk + 1) * LANES)
            low_at = slice(NEAR + at.start, NEAR + at.stop)
            rx, ry, rz = (npos[s, a : a + 1, at] - post[own, a : a + 1] for a in range(3))
            squared = rx * rx + ry * ry + rz * rz + SOFTENING * SOFTENING
            inverse = lax.rsqrt(squared)
            distance = squared * inverse
            keep = distance < CUTOFF
            if chunk == 0:
                lane = lax.broadcasted_iota(jnp.int32, (SLOTS, LANES), 1)
                slot = lax.broadcasted_iota(jnp.int32, (SLOTS, LANES), 0)
                keep = keep & (lane != slot + s * SLOTS)
            values, slopes = radial_parts(distance, inverse, keep)
            ux, uy, uz = rx * inverse, ry * inverse, rz * inverse
            for a, part in enumerate((ux, uy, uz, inverse)):
                geo[s, a, :, at] = part
            harmonic = harmonics(ux, uy, uz)
            for n in range(BASIS):
                rad[s, n, :, at] = values[n]
                rad[s, BASIS + n, :, at] = slopes[n]
                for m in range(9):
                    value = values[n] if m == 0 else values[n] * harmonic[m]
                    high, low = halves(value)
                    rows = slice((n * 9 + m) * SLOTS, (n * 9 + m + 1) * SLOTS)
                    pair[rows, at] = high
                    pair[rows, low_at] = low
        mom[...] = dot(pair[...], fcat[s])
        for m in range(9):
            total = None
            for n in range(BASIS):
                rows = slice((n * 9 + m) * SLOTS, (n * 9 + m + 1) * SLOTS)
                l = DEGREE_OF[m]
                term = (mom[rows, 0:128] + mom[rows, 128:256]) * radial_ref[l, n : n + 1, :]
                total = term if total is None else total + term
            summed[m, own, :] = total
        return carry

    lax.fori_loop(0, 8, forward, 0)

    slot = lax.broadcasted_iota(jnp.int32, (SLOTS, LANES), 0)
    occupied = jnp.concatenate(
        [jnp.where(slot < counts_ref[x, y, z], 1.0, 0.0) for x, y, z in CELLS], axis=0
    )
    mixed = []
    for l, span in enumerate((slice(0, 1), slice(1, 4), slice(4, 9))):
        part = summed[span].reshape((span.stop - span.start) * LANES, LANES)
        part = dot_split(part, mix_ref[l])
        mixed += [part[i * LANES : (i + 1) * LANES] for i in range(span.stop - span.start)]
    q0 = mixed[0]
    q1 = sum(v * v for v in mixed[1:4])
    q2 = sum(v * v for v in mixed[4:9])
    r0, r1, r2, r3 = (readout_ref[i : i + 1, :] for i in range(4))
    layer = q0 * r0 + q1 * r1 + q2 * r2 + (q0 * q1) * r3
    layer = jnp.sum(jnp.transpose(layer), axis=0, keepdims=True)
    lane16 = lax.broadcasted_iota(jnp.int32, (1, SLOTS), 1)
    for q, (x, y, z) in enumerate(CELLS):
        kind = species_ref[x, y, z : z + 1, :]
        value = layer[:, q * SLOTS : (q + 1) * SLOTS]
        for k in range(table_ref.shape[0]):
            value = value + jnp.where(kind == k, table_ref[k], 0.0)
        energy_ref[x, y, z : z + 1, :] = jnp.where(lane16 < counts_ref[x, y, z], value, 0.0)
    slope1 = 2.0 * occupied * (r1 + q0 * r3)
    slope2 = 2.0 * occupied * r2
    back = [occupied * (r0 + q1 * r3)]
    back += [v * slope1 for v in mixed[1:4]]
    back += [v * slope2 for v in mixed[4:9]]
    for l, span in enumerate((slice(0, 1), slice(1, 4), slice(4, 9))):
        part = dot_split(jnp.concatenate(back[span], axis=0), mix_ref[l], 1)
        summed[span] = part.reshape(span.stop - span.start, LANES, LANES)

    def backward(s, carry):
        own = pl.ds(pl.multiple_of(s * SLOTS, SLOTS), SLOTS)
        for m in range(9):
            slope = summed[m, own, :]
            l = DEGREE_OF[m]
            for n in range(BASIS):
                rows = slice((n * 9 + m) * SLOTS, (n * 9 + m + 1) * SLOTS)
                high, low = halves(slope * radial_ref[l, n : n + 1, :])
                gpair[rows, 0:128] = high
                gpair[rows, 128:256] = low
                gpair[rows, 256:384] = high
        dpair[...] = dot(gpair[...], fback[s], 1)
        pull = [None] * 3
        for chunk in range(CHUNKS):
            at = slice(chunk * LANES, (chunk + 1) * LANES)
            ux, uy, uz, inverse = (geo[s, a, :, at] for a in range(4))
            harmonic = harmonics(ux, uy, uz)
            amp = [None] * 9
            along = None
            for n in range(BASIS):
                value, slope = rad[s, n, :, at], rad[s, BASIS + n, :, at]
                inner = None
                for m in range(9):
                    part = dpair[(n * 9 + m) * SLOTS : (n * 9 + m + 1) * SLOTS, at]
                    if m > 0:
                        amp[m] = part * value if n == 0 else amp[m] + part * value
                    inner = part if m == 0 else inner + part * harmonic[m]
                along = inner * slope if n == 0 else along + inner * slope
            vx = R3 * amp[1] + R15 * (uy * amp[4] + uz * amp[7] + ux * amp[8]) - R5 * (ux * amp[6])
            vy = R3 * amp[2] + R15 * (ux * amp[4] + uz * amp[5] - uy * amp[8]) - R5 * (uy * amp[6])
            vz = R3 * amp[3] + R15 * (uy * amp[5] + ux * amp[7]) + (2.0 * R5) * (uz * amp[6])
            radial = along - inverse * (ux * vx + uy * vy + uz * vz)
            for a, (u, v) in enumerate(((ux, vx), (uy, vy), (uz, vz))):
                slope = u * radial + inverse * v
                ngrad[s, a : a + 1, at] = jnp.sum(slope, axis=0, keepdims=True)
                pull[a] = slope if chunk == 0 else pull[a] + slope
        for a in range(3):
            center[a, own, :] = pull[a]
        return carry

    lax.fori_loop(0, 8, backward, 0)

    grads_ref[...] = jnp.zeros_like(grads_ref)
    for a in range(3):
        grads_ref[SELF, a : a + 1, :] = -jnp.sum(jnp.transpose(center[a]), axis=0, keepdims=True)
    for s in range(8):
        for chunk in range(CHUNKS):
            whole = ngrad[s, :, chunk * LANES : (chunk + 1) * LANES]
            for (domain, turn), places in grouped(TABLES[s], chunk):
                piece = whole if len(places) == 8 else jnp.where(places_mask(places), whole, 0.0)
                if turn:
                    piece = pltpu.roll(piece, (8 - turn) * SLOTS, 1)
                grads_ref[domain] = grads_ref[domain] + piece


def return_kernel(grads_ref, force_ref, landed, sends, recvs):
    barrier = greet()
    pl.semaphore_wait(barrier, 26)
    copies = []
    for domain in range(27):
        if domain != SELF:
            copies.append(
                pltpu.make_async_remote_copy(
                    grads_ref.at[domain], landed.at[26 - domain], sends.at[domain],
                    recvs.at[26 - domain], device_id=neighbour(domain), device_id_type=MESH,
                )
            )
    for copy in copies:
        copy.start()
    for copy in copies:
        copy.wait()
    total = grads_ref[SELF]
    for domain in range(27):
        if domain != SELF:
            total = total + landed[domain]
    total = -total
    for q, (x, y, z) in enumerate(CELLS):
        force_ref[x, y, :, z, :] = total[0:3, q * SLOTS : (q + 1) * SLOTS]


VMEM = pl.BlockSpec(memory_space=pltpu.VMEM)
SMEM = pl.BlockSpec(memory_space=pltpu.SMEM)
ANY = pl.BlockSpec(memory_space=pl.ANY)


def halo(positions, features, counts):
    return pl.pallas_call(
        halo_kernel,
        out_shape=(
            jax.ShapeDtypeStruct((27, 8, LANES), F32),
            jax.ShapeDtypeStruct((27, 2, 2, 2, SLOTS, LANES), F32),
        ),
        in_specs=[VMEM, VMEM, SMEM],
        out_specs=(ANY, ANY),
        scratch_shapes=[
            pltpu.VMEM((8, LANES), F32),
            pltpu.VMEM((2, 2, 2, SLOTS, LANES), F32),
            pltpu.SemaphoreType.DMA((2, 27)),
            pltpu.SemaphoreType.DMA((2, 27)),
            pltpu.SemaphoreType.DMA((2,)),
        ],
        compiler_params=pltpu.CompilerParams(collective_id=0, has_side_effects=True),
    )(positions, features, counts)


def cell_forces(tiles, feats, species, counts, table, radial, mix, readout):
    return pl.pallas_call(
        force_kernel,
        out_shape=(
            jax.ShapeDtypeStruct((2, 2, 2, SLOTS), F32),
            jax.ShapeDtypeStruct((27, 8, LANES), F32),
        ),
        in_specs=[VMEM, VMEM, VMEM, SMEM, SMEM, VMEM, VMEM, VMEM],
        out_specs=(VMEM, VMEM),
        scratch_shapes=[
            pltpu.VMEM((8, 8, NEAR), F32),
            pltpu.VMEM((LANES, LANES), F32),
            pltpu.VMEM((8, 2 * NEAR, 256), BF16),
            pltpu.VMEM((8, NEAR, 384), BF16),
            pltpu.VMEM((ROWS, 2 * NEAR), BF16),
            pltpu.VMEM((ROWS, 256), F32),
            pltpu.VMEM((9, LANES, LANES), F32),
            pltpu.VMEM((8, 2 * BASIS, SLOTS, NEAR), F32),
            pltpu.VMEM((8, 4, SLOTS, NEAR), F32),
            pltpu.VMEM((ROWS, 384), BF16),
            pltpu.VMEM((ROWS, NEAR), F32),
            pltpu.VMEM((8, 8, NEAR), F32),
            pltpu.VMEM((3, LANES, LANES), F32),
        ],
        compiler_params=pltpu.CompilerParams(vmem_limit_bytes=48 * 2**20),
    )(tiles, feats, species, counts, table, radial, mix, readout)


def give_back(grads):
    return pl.pallas_call(
        return_kernel,
        out_shape=jax.ShapeDtypeStruct((2, 2, 3, 2, SLOTS), F32),
        in_specs=[VMEM],
        out_specs=VMEM,
        scratch_shapes=[
            pltpu.VMEM((27, 8, LANES), F32),
            pltpu.SemaphoreType.DMA((27,)),
            pltpu.SemaphoreType.DMA((27,)),
        ],
        compiler_params=pltpu.CompilerParams(collective_id=1, has_side_effects=True),
    )(grads)


def per_device(positions, features, species, counts, species_energy, radial_weight, mix_weight, readout):
    tiles, feats = halo(jnp.swapaxes(positions, 2, 3), features, counts)
    feats = feats.reshape(27 * 8, SLOTS, LANES)
    energies, grads = cell_forces(
        tiles, feats, species, counts, species_energy, jnp.swapaxes(radial_weight, 0, 1),
        mix_weight, readout,
    )
    return energies, jnp.swapaxes(give_back(grads), 2, 3)


def solution(mesh):
    grid = P("gx", "gy", "gz")
    return jax.shard_map(
        per_device,
        mesh=mesh,
        in_specs=(grid, grid, grid, grid, P(), P(), P(), P()),
        out_specs=(grid, grid),
        check_vma=False,
    )
```

time: 399 us -> 69.3 us (0.17); the launches traced: 391 us -> 68.8 us
  other arithmetic: 107 us -> 0 us
  local copies, waits for them, and re-layouts: 97.8 us -> 8.65 us
  starting transfers between devices: 75.3 us -> 0 us
  matrix products: 74.6 us -> 0 us
  Pallas kernels: 0 us -> 59.5 us
  loops' own time: 24.7 us -> 0 us
  waiting for transfers between devices: 10.3 us -> 0 us
    ppermute x18 -> x0, starting transfers between devices: 75.3 us -> none  [the longest x9 42.7 us: with_halo(): lax.ppermute(lax.slice_in_dim(block, 0, width, axis=dim), axis, backward)]
    dot_general x80 -> x0, matrix products: 64 us -> none  [the longest x16 43.4 us: cell_energy(): jnp.einsum('nmik,kc->inmc', pair_tiles, near_feat, precision=highest)]
    dynamic_update_slice x64 -> x0, other arithmetic: 61 us -> none  [the longest x56 44.7 us: local_energies(): result = lax.map(one_cell, cell_ids)]
    pallas_call x0 -> x3, Pallas kernels: none -> 59.5 us  [the longest x1 28 us: halo(): pl.pallas_call(halo_kernel, out_shape=(jax.ShapeDtypeStruct((27, 8, LANES...]
    another operation x2 -> x0, loops' own time: 24.7 us -> none  [local_energies(): result = lax.map(one_cell, cell_ids)]
    dynamic_update_slice x72 -> x0, local copies, waits for them, and re-layouts: 24.2 us -> none  [local_energies(): result = lax.map(one_cell, cell_ids)]
    mul x24 -> x0, local copies, waits for them, and re-layouts: 22 us -> none  [the longest x16 15.7 us: cell_energy(): pair_tiles = radial[:, None] * harmonic[None]]
    dynamic_slice x48 -> x0, local copies, waits for them, and re-layouts: 20.9 us -> none  [the longest x32 20.5 us: local_energies(): result = lax.map(one_cell, cell_ids)]
  transfers between devices with their start and end apart: 18 -> 0, of which waited for: 5 -> 0; matrix products, arithmetic and copies ran while one was open for 2% -> 0% of each run, Pallas kernels for 0% -> 0%
where the time goes in v1:
time: 69.3 us; the launch traced here: 68.8 us
  Pallas kernels  59.5 us (86%)
  local copies, waits for them, and re-layouts  8.65 us (12%)
    pallas_call x1, Pallas kernels, halo(): pl.pallas_call(halo_kernel, out_shape=(jax.ShapeDtypeStruct((27, 8, LANES...  28 us
    pallas_call x1, Pallas kernels, cell_forces(): pl.pallas_call(force_kernel, out_shape=(jax.ShapeDtypeStruct((2, 2, 2, SL...  18.9 us
    pallas_call x1, Pallas kernels, give_back(): pl.pallas_call(return_kernel, out_shape=jax.ShapeDtypeStruct((2, 2, 3, 2,...  12.6 us
    unnamed x19, local copies, waits for them, and re-layouts  8.65 us

profile of v1, /device:TPU:1, one launch (start us, length us, event | category | flops | bytes accessed | tf_op | source)
XLA Modules:
  0.0 68.8 jit_solution(4617796938811997047)
XLA Ops:
  0.6 28.0 %shard_map.95 = (f32[27,8,128]{2,1,0:T(8,128)}, f32[27,2,2,2,16,128]{5,4,3,2,1,0:T(8,128)}) custom-call(f32[2,2,3,2,16]{4,3,2,1,0:T(2,128)} %bitcast.7, f32[2,2,2,16,128]{4,3,2,1,0:T(8,128)} %feat_ref.1, s32[2,2,2]{2,1,0:T(2,128)} %counts_ref.3), custom_call_target="tpu_custom_call" | custom-call | tf_op jit(solution)/shard_map/pallas_call | solution.py:412
  28.7 0.0 copy-start
  28.7 1.5 %copy-done = f32[27,2,2,2,16,128]{5,4,3,2,1,0:T(8,128)S(1)} copy-done((f32[27,2,2,2,16,128]{5,4,3,2,1,0:T(8,128)S(1)}, f32[27,2,2,2,16,128]{5,4,3,2,1,0:T(8,128)}, u32[]{:S(2)}) %copy-start) | copy-done | bytes 1769496
  30.2 0.0 copy-start.1
  30.2 0.9 %copy-done.1 = f32[3,128,128]{2,1,0:T(8,128)S(1)} copy-done((f32[3,128,128]{2,1,0:T(8,128)S(1)}, f32[3,128,128]{2,1,0:T(8,128)}, u32[]{:S(2)}) %copy-start.1) | copy-done | bytes 196632
  31.1 0.0 copy-start.3
  31.1 0.9 %copy-done.3 = f32[27,8,128]{2,1,0:T(8,128)S(1)} copy-done((f32[27,8,128]{2,1,0:T(8,128)S(1)}, f32[27,8,128]{2,1,0:T(8,128)}, u32[]{:S(2)}) %copy-start.3) | copy-done | bytes 110616
  32.0 0.0 copy-start.4
  32.0 0.7 %copy-done.4 = f32[8,3,128]{2,0,1:T(8,128)S(1)} copy-done((f32[8,3,128]{2,0,1:T(8,128)S(1)}, f32[8,3,128]{2,0,1:T(8,128)}, u32[]{:S(2)}) %copy-start.4) | copy-done | bytes 12312
  32.7 0.0 copy-start.5
  32.7 0.7 copy-done.5
  33.4 0.0 copy-start.6
  33.4 0.7 copy-done.6
  34.1 0.0 copy-start.7
  34.1 0.7 copy-done.7
  34.7 0.0 copy-start.8
  34.8 0.7 copy-done.8
  35.4 18.9 %shard_map.96 = (f32[2,2,2,16]{3,2,1,0:T(2,128)}, f32[27,8,128]{2,1,0:T(8,128)S(1)}) custom-call(f32[27,8,128]{2,1,0:T(8,128)S(1)} %copy-done.3, f32[216,16,128]{2,1,0:T(8,128)S(1)} %bitcast.4, s32[2,2,2,16]{3,2,1,0:T(2,128)S(1)} %copy-done.6, s32[2,2,2]{2,1,0:T(2,128)S(1)} %copy-done.5, f32[10]{0:T(128)S(1)} %copy-done.8, f32[3,8,128]{2,1,0:T(8,128)S(1)} %bitcast.5, ...), custom_call_target="tpu_custom_call" | custom-call | tf_op jit(solution)/shard_map/pallas_call | solution.py:432
  54.3 0.0 copy-start.2
  54.3 0.6 copy-done.2
  54.9 12.6 %shard_map.97 = f32[2,2,3,2,16]{4,3,2,1,0:T(2,128)} custom-call(f32[27,8,128]{2,1,0:T(8,128)} %copy-done.2), custom_call_target="tpu_custom_call" | custom-call | tf_op jit(solution)/shard_map/pallas_call | solution.py:460
  67.5 1.3 %copy.11 = f32[2,2,2,3,16]{4,2,3,1,0:T(2,128)} copy(f32[2,2,2,3,16]{4,2,3,1,0:T(2,128)} %bitcast.6) | data formatting | bytes 3072
Async XLA Ops:
  28.7 1.5 %copy-start = (f32[27,2,2,2,16,128]{5,4,3,2,1,0:T(8,128)S(1)}, f32[27,2,2,2,16,128]{5,4,3,2,1,0:T(8,128)}, u32[]{:S(2)}) copy-start(f32[27,2,2,2,16,128]{5,4,3,2,1,0:T(8,128)} %get-tuple-element.7) | copy-start | bytes 5308420
  30.2 0.9 %copy-start.1 = (f32[3,128,128]{2,1,0:T(8,128)S(1)}, f32[3,128,128]{2,1,0:T(8,128)}, u32[]{:S(2)}) copy-start(f32[3,128,128]{2,1,0:T(8,128)} %mix_ref.1) | copy-start | bytes 589828
  31.1 0.9 %copy-start.3 = (f32[27,8,128]{2,1,0:T(8,128)S(1)}, f32[27,8,128]{2,1,0:T(8,128)}, u32[]{:S(2)}) copy-start(f32[27,8,128]{2,1,0:T(8,128)} %get-tuple-element.6.tiles_ref) | copy-start | bytes 331780
  32.0 0.7 %copy-start.4 = (f32[8,3,128]{2,0,1:T(8,128)S(1)}, f32[8,3,128]{2,0,1:T(8,128)}, u32[]{:S(2)}) copy-start(f32[8,3,128]{2,0,1:T(8,128)} %param.13) | copy-start | bytes 36868
  32.7 0.7 copy-start.5
  33.4 0.7 copy-start.6
  34.1 0.7 copy-start.7
  34.7 0.7 copy-start.8
  54.3 0.6 copy-start.2

commit v2 on v1

v2 whole, which is shorter than its diff:
```python
import math

import jax
import jax.numpy as jnp
import numpy as np
from jax import lax
from jax.experimental import pallas as pl
from jax.experimental.pallas import tpu as pltpu
from jax.sharding import PartitionSpec as P

CUTOFF = 5.0
CELL_SIDE = 5.0
SOFTENING = 0.5
BASIS = 8
SLOTS = 16
LANES = 128
CHUNKS = 4
NEAR = CHUNKS * LANES
GHOST = NEAR - LANES
ROWS = BASIS * 9 * SLOTS
DEGREE_OF = (0, 1, 1, 1, 2, 2, 2, 2, 2)
SELF = 13
MESH = pl.DeviceIdType.MESH
AXES = ("gx", "gy", "gz")
R3, R5, R15 = math.sqrt(3.0), math.sqrt(5.0), math.sqrt(15.0)
F32, BF16 = jnp.float32, jnp.bfloat16

OFFSETS = [(a, b, c) for a in (-1, 0, 1) for b in (-1, 0, 1) for c in (-1, 0, 1)]
CELLS = [(x, y, z) for x in (0, 1) for y in (0, 1) for z in (0, 1)]


def near_table(cell):
    sign = [1 if c == 1 else -1 for c in cell]
    rim = [0 if s == 1 else 1 for s in sign]
    taken = {(0, q) for q in range(8)}
    table = [(0, q, SELF, q) for q in range(8)]
    late = []
    for size in (1, 2, 3):
        for subset in range(1, 8):
            dims = [d for d in range(3) if subset >> d & 1]
            if len(dims) != size:
                continue
            off = [sign[d] if d in dims else 0 for d in range(3)]
            domain = OFFSETS.index(tuple(off))
            for q, coords in enumerate(CELLS):
                if any(coords[d] != rim[d] for d in dims):
                    continue
                for chunk in range(1, CHUNKS):
                    if (chunk, q) not in taken:
                        taken.add((chunk, q))
                        table.append((chunk, q, domain, q))
                        break
                else:
                    late.append((domain, q))
    for domain, q in late:
        chunk, place = min(
            (c, p) for c in range(1, CHUNKS) for p in range(8) if (c, p) not in taken
        )
        taken.add((chunk, place))
        table.append((chunk, place, domain, q))
    return table


TABLES = [near_table(cell) for cell in CELLS]


def grouped(table, chunk):
    groups = {}
    for c, place, domain, q in table:
        if c == chunk:
            groups.setdefault((domain, (place - q) % 8), []).append(place)
    return sorted(groups.items())


def places_mask(places):
    lane = lax.broadcasted_iota(jnp.int32, (8, LANES), 1)
    mask = None
    for place in places:
        one = (lane >= place * SLOTS) & (lane < (place + 1) * SLOTS)
        mask = one if mask is None else mask | one
    return mask


def neighbour(domain):
    place = []
    for axis, step in zip(AXES, OFFSETS[domain]):
        count = lax.axis_size(axis)
        place.append(lax.rem(lax.axis_index(axis) + step + count, count))
    return tuple(place)


def rim_of(domain):
    return tuple(
        pl.ds(0, 2) if step == 0 else pl.ds(1 if step == 1 else 0, 1) for step in OFFSETS[domain]
    )


def greet():
    barrier = pltpu.get_barrier_semaphore()
    for domain in range(27):
        if domain != SELF:
            pl.semaphore_signal(
                barrier, inc=1, device_id=neighbour(domain), device_id_type=MESH
            )
    return barrier


def halves(value):
    high = value.astype(BF16)
    return high, (value - high.astype(F32)).astype(BF16)


def dot(a, b, rhs_dim=0):
    return lax.dot_general(
        a, b, (((1,), (rhs_dim,)), ((), ())), preferred_element_type=F32
    )


def dot_split(a, b, rhs_dim=0):
    a_high, a_low = halves(a)
    b_high, b_low = halves(b)
    return (
        dot(a_low, b_high, rhs_dim) + dot(a_high, b_low, rhs_dim) + dot(a_high, b_high, rhs_dim)
    )


def harmonics(ux, uy, uz):
    square = ux * ux + uy * uy + uz * uz
    return [
        None,
        R3 * ux,
        R3 * uy,
        R3 * uz,
        R15 * ux * uy,
        R15 * uy * uz,
        0.5 * R5 * (3.0 * uz * uz - square),
        R15 * ux * uz,
        0.5 * R15 * (ux * ux - uy * uy),
    ]


def radial_parts(distance, inverse, keep):
    t = jnp.minimum(distance * (1.0 / CUTOFF), 1.0)
    phi = math.pi * (t - 0.5)
    sq = phi * phi
    sine, cosine = 0.0, 0.0
    for k in range(6, -1, -1):
        if k < 6:
            sine = sine * sq + (-1) ** k / math.factorial(2 * k + 1)
        cosine = cosine * sq + (-1) ** k / math.factorial(2 * k)
    s1, c1 = cosine, -(sine * phi)
    t2 = t * t
    t4 = t2 * t2
    env = jnp.where(keep, 1.0 + t4 * t * (-21.0 + t * (35.0 - 15.0 * t)), 0.0)
    gap = 1.0 - t
    env_d = jnp.where(keep, (-105.0 / CUTOFF) * t4 * gap * gap, 0.0)
    scale = math.sqrt(2.0 / CUTOFF)
    w = scale * env * inverse
    w_d = inverse * (scale * env_d - w)
    twice = 2.0 * c1
    sines, cosines = [s1], [c1]
    for n in range(1, BASIS):
        sines.append(twice * sines[-1] - (sines[-2] if n > 1 else 0.0))
        cosines.append(twice * cosines[-1] - (cosines[-2] if n > 1 else 1.0))
    values = [s * w for s in sines]
    slopes = [
        ((n + 1) * math.pi / CUTOFF) * (c * w) + s * w_d
        for n, (s, c) in enumerate(zip(sines, cosines))
    ]
    return values, slopes


def near_pairs(s, chunk, npos, post, geo, rad, pair, high_at, low_at):
    own = pl.ds(pl.multiple_of(s * SLOTS, SLOTS), SLOTS)
    at = slice(chunk * LANES, (chunk + 1) * LANES)
    rx, ry, rz = (npos[s, a : a + 1, at] - post[own, a : a + 1] for a in range(3))
    squared = rx * rx + ry * ry + rz * rz + SOFTENING * SOFTENING
    inverse = lax.rsqrt(squared)
    distance = squared * inverse
    keep = distance < CUTOFF
    if chunk == 0:
        lane = lax.broadcasted_iota(jnp.int32, (SLOTS, LANES), 1)
        slot = lax.broadcasted_iota(jnp.int32, (SLOTS, LANES), 0)
        keep = keep & (lane != slot + s * SLOTS)
    values, slopes = radial_parts(distance, inverse, keep)
    ux, uy, uz = rx * inverse, ry * inverse, rz * inverse
    for a, part in enumerate((ux, uy, uz, inverse)):
        geo[s, a, :, at] = part
    harmonic = harmonics(ux, uy, uz)
    for n in range(BASIS):
        rad[s, n, :, at] = values[n]
        rad[s, BASIS + n, :, at] = slopes[n]
        for m in range(9):
            high, low = halves(values[n] if m == 0 else values[n] * harmonic[m])
            rows = slice((n * 9 + m) * SLOTS, (n * 9 + m + 1) * SLOTS)
            pair[rows, high_at : high_at + LANES] = high
            pair[rows, low_at : low_at + LANES] = low


def weighted(mom, radial, m):
    total = None
    for n in range(BASIS):
        rows = slice((n * 9 + m) * SLOTS, (n * 9 + m + 1) * SLOTS)
        l = DEGREE_OF[m]
        term = (mom[rows, 0:128] + mom[rows, 128:256]) * radial[l, n : n + 1, :]
        total = term if total is None else total + term
    return total


def put_near(s, chunk, npos, tiles):
    row = lax.broadcasted_iota(jnp.int32, (8, LANES), 0)
    value = jnp.full((8, LANES), 100.0, F32)
    for (domain, turn), places in grouped(TABLES[s], chunk):
        ox, oy, oz = (2.0 * CELL_SIDE * o for o in OFFSETS[domain])
        piece = tiles[domain]
        if domain != SELF:
            piece = piece + jnp.where(row == 0, ox, jnp.where(row == 1, oy, oz))
        if turn:
            piece = pltpu.roll(piece, turn * SLOTS, 1)
        value = piece if len(places) == 8 else jnp.where(places_mask(places), piece, value)
    npos[s, :, chunk * LANES : (chunk + 1) * LANES] = value


def put_features(high, low, fcat, s, at, low_by, fback, back_at):
    rows, low_rows = slice(at, at + SLOTS), slice(at + low_by, at + low_by + SLOTS)
    where = () if s is None else (s,)
    fcat[where + (rows, slice(0, 128))] = high
    fcat[where + (rows, slice(128, 256))] = low
    fcat[where + (low_rows, slice(0, 128))] = high
    fcat[where + (low_rows, slice(128, 256))] = jnp.zeros_like(low)
    for b in range(8) if s is None else (s,):
        rows = slice(back_at, back_at + SLOTS)
        fback[b, rows, 0:128] = high
        fback[b, rows, 128:256] = high
        fback[b, rows, 256:384] = low


def whole_kernel(
    pos_hbm, feat_hbm, species_hbm, counts_hbm, table_hbm, radial_hbm, mix_hbm, readout_hbm,
    energy_ref, force_ref,
    pos, feat, species, counts, table, radial, mix, readout, loads,
    tiles, feats, sends, recvs, landed, back_sends, back_recvs,
    npos, post, fown, fcat, fback, opair, pair, mom, summed, rad, geo, gpair, dpair, ngrad, center,
    grads,
):
    barrier = greet()
    held = [
        pltpu.make_async_copy(source, target, loads.at[i])
        for i, (source, target) in enumerate(
            (
                (pos_hbm, pos), (counts_hbm, counts), (feat_hbm, feat), (radial_hbm, radial),
                (mix_hbm, mix), (readout_hbm, readout), (species_hbm, species), (table_hbm, table),
            )
        )
    ]
    for copy in held:
        copy.start()
    slot = lax.broadcasted_iota(jnp.int32, (SLOTS, LANES), 0)
    tiles[SELF] = jnp.zeros((8, LANES), F32)
    ngrad[...] = jnp.zeros_like(ngrad)
    grads[...] = jnp.zeros_like(grads)
    for copy in held[:3]:
        copy.wait()
    for q, (x, y, z) in enumerate(CELLS):
        tiles[SELF, 0:3, q * SLOTS : (q + 1) * SLOTS] = pos[x, y, :, z, :]
        occupied = slot < counts[x, y : y + 1, z : z + 1]
        feats[SELF, x, y, z] = jnp.where(occupied, feat[x, y, z], 0.0)
    lane = lax.broadcasted_iota(jnp.int32, (8, LANES), 1)
    row = lax.broadcasted_iota(jnp.int32, (8, LANES), 0)
    shift = jnp.where(row == 0, lane // 64, jnp.where(row == 1, lane // 32 % 2, lane // 16 % 2))
    tiles[SELF] = tiles[SELF] + CELL_SIDE * shift.astype(F32)

    copies = []
    for domain in range(27):
        if domain == SELF:
            continue
        there, rim, back = neighbour(domain), rim_of(domain), 26 - domain
        copies.append(
            pltpu.make_async_remote_copy(
                tiles.at[SELF], tiles.at[back], sends.at[0, domain], recvs.at[0, back],
                device_id=there, device_id_type=MESH,
            )
        )
        copies.append(
            pltpu.make_async_remote_copy(
                feats.at[(SELF,) + rim], feats.at[(back,) + rim], sends.at[1, domain],
                recvs.at[1, back], device_id=there, device_id_type=MESH,
            )
        )
    pl.semaphore_wait(barrier, 26)
    for copy in copies:
        copy.start()

    for s in range(8):
        put_near(s, 0, npos, tiles)
    mine = tiles[SELF]
    post[...] = jnp.transpose(jnp.concatenate([mine] * 16, axis=0))
    for q, (x, y, z) in enumerate(CELLS):
        high, low = halves(feats[SELF, x, y, z])
        put_features(high, low, fown, None, q * SLOTS, LANES, fback, q * SLOTS)
    for copy in held[3:]:
        copy.wait()

    def inside(s, carry):
        near_pairs(s, 0, npos, post, geo, rad, opair, 0, LANES)
        mom[...] = dot(opair[...], fown[...])
        own = pl.ds(pl.multiple_of(s * SLOTS, SLOTS), SLOTS)
        for m in range(9):
            summed[m, own, :] = weighted(mom, radial, m)
        return carry

    lax.fori_loop(0, 8, inside, 0)

    for copy in copies:
        copy.wait()
    for s in range(8):
        for chunk in range(1, CHUNKS):
            put_near(s, chunk, npos, tiles)
        filled = {(c, p): (domain, q) for c, p, domain, q in TABLES[s]}
        for chunk in range(1, CHUNKS):
            for place in range(8):
                at = (chunk - 1) * LANES + place * SLOTS
                if (chunk, place) in filled:
                    domain, q = filled[(chunk, place)]
                    high, low = halves(feats[(domain,) + CELLS[q]])
                else:
                    high = low = jnp.zeros((SLOTS, LANES), BF16)
                put_features(high, low, fcat, s, at, GHOST, fback, at + LANES)

    def outside(s, carry):
        for chunk in range(1, CHUNKS):
            at = (chunk - 1) * LANES
            near_pairs(s, chunk, npos, post, geo, rad, pair, at, GHOST + at)
        mom[...] = dot(pair[...], fcat[s])
        own = pl.ds(pl.multiple_of(s * SLOTS, SLOTS), SLOTS)
        for m in range(9):
            summed[m, own, :] = summed[m, own, :] + weighted(mom, radial, m)
        return carry

    lax.fori_loop(0, 8, outside, 0)

    occupied = jnp.concatenate(
        [jnp.where(slot < counts[x, y : y + 1, z : z + 1], 1.0, 0.0) for x, y, z in CELLS], axis=0
    )
    mixed = []
    for l, span in enumerate((slice(0, 1), slice(1, 4), slice(4, 9))):
        part = summed[span].reshape((span.stop - span.start) * LANES, LANES)
        part = dot_split(part, mix[l])
        mixed += [part[i * LANES : (i + 1) * LANES] for i in range(span.stop - span.start)]
    q0 = mixed[0]
    q1 = sum(v * v for v in mixed[1:4])
    q2 = sum(v * v for v in mixed[4:9])
    r0, r1, r2, r3 = (readout[i : i + 1, :] for i in range(4))
    layer = q0 * r0 + q1 * r1 + q2 * r2 + (q0 * q1) * r3
    layer = jnp.sum(jnp.transpose(layer), axis=0, keepdims=True)
    lane16 = lax.broadcasted_iota(jnp.int32, (1, SLOTS), 1)
    for q, (x, y, z) in enumerate(CELLS):
        kind = species[x, y, z : z + 1, :]
        value = layer[:, q * SLOTS : (q + 1) * SLOTS]
        for k in range(table.shape[0]):
            value = value + jnp.where(kind == k, table[k], 0.0)
        energy_ref[x, y, z : z + 1, :] = jnp.where(lane16 < counts[x, y : y + 1, z : z + 1], value, 0.0)
    slope1 = 2.0 * occupied * (r1 + q0 * r3)
    slope2 = 2.0 * occupied * r2
    back = [occupied * (r0 + q1 * r3)]
    back += [v * slope1 for v in mixed[1:4]]
    back += [v * slope2 for v in mixed[4:9]]
    for l, span in enumerate((slice(0, 1), slice(1, 4), slice(4, 9))):
        part = dot_split(jnp.concatenate(back[span], axis=0), mix[l], 1)
        summed[span] = part.reshape(span.stop - span.start, LANES, LANES)

    def backward(s, carry):
        own = pl.ds(pl.multiple_of(s * SLOTS, SLOTS), SLOTS)
        for m in range(9):
            slope = summed[m, own, :]
            l = DEGREE_OF[m]
            for n in range(BASIS):
                rows = slice((n * 9 + m) * SLOTS, (n * 9 + m + 1) * SLOTS)
                high, low = halves(slope * radial[l, n : n + 1, :])
                gpair[rows, 0:128] = high
                gpair[rows, 128:256] = low
                gpair[rows, 256:384] = high
        dpair[...] = dot(gpair[...], fback[s], 1)
        pull = [None] * 3
        for chunk in range(CHUNKS):
            at = slice(chunk * LANES, (chunk + 1) * LANES)
            ux, uy, uz, inverse = (geo[s, a, :, at] for a in range(4))
            harmonic = harmonics(ux, uy, uz)
            amp = [None] * 9
            along = None
            for n in range(BASIS):
                value, slope = rad[s, n, :, at], rad[s, BASIS + n, :, at]
                inner = None
                for m in range(9):
                    part = dpair[(n * 9 + m) * SLOTS : (n * 9 + m + 1) * SLOTS, at]
                    if m > 0:
                        amp[m] = part * value if n == 0 else amp[m] + part * value
                    inner = part if m == 0 else inner + part * harmonic[m]
                along = inner * slope if n == 0 else along + inner * slope
            vx = R3 * amp[1] + R15 * (uy * amp[4] + uz * amp[7] + ux * amp[8]) - R5 * (ux * amp[6])
            vy = R3 * amp[2] + R15 * (ux * amp[4] + uz * amp[5] - uy * amp[8]) - R5 * (uy * amp[6])
            vz = R3 * amp[3] + R15 * (uy * amp[5] + ux * amp[7]) + (2.0 * R5) * (uz * amp[6])
            central = along - inverse * (ux * vx + uy * vy + uz * vz)
            for a, (u, v) in enumerate(((ux, vx), (uy, vy), (uz, vz))):
                slope = u * central + inverse * v
                ngrad[s, a : a + 1, at] = jnp.sum(slope, axis=0, keepdims=True)
                pull[a] = slope if chunk == 0 else pull[a] + slope
        for a in range(3):
            center[a, own, :] = pull[a]
        return carry

    lax.fori_loop(0, 8, backward, 0)

    for a in range(3):
        grads[SELF, a : a + 1, :] = -jnp.sum(jnp.transpose(center[a]), axis=0, keepdims=True)
    for s in range(8):
        for chunk in range(CHUNKS):
            whole = ngrad[s, :, chunk * LANES : (chunk + 1) * LANES]
            for (domain, turn), places in grouped(TABLES[s], chunk):
                piece = whole if len(places) == 8 else jnp.where(places_mask(places), whole, 0.0)
                if turn:
                    piece = pltpu.roll(piece, (8 - turn) * SLOTS, 1)
                grads[domain] = grads[domain] + piece

    copies = []
    for domain in range(27):
        if domain != SELF:
            copies.append(
                pltpu.make_async_remote_copy(
                    grads.at[domain], landed.at[26 - domain], back_sends.at[domain],
                    back_recvs.at[26 - domain], device_id=neighbour(domain), device_id_type=MESH,
                )
            )
    for copy in copies:
        copy.start()
    for copy in copies:
        copy.wait()
    total = grads[SELF]
    for domain in range(27):
        if domain != SELF:
            total = total + landed[domain]
    total = -total
    for q, (x, y, z) in enumerate(CELLS):
        force_ref[x, y, :, z, :] = total[0:3, q * SLOTS : (q + 1) * SLOTS]


VMEM = pl.BlockSpec(memory_space=pltpu.VMEM)
HBM = pl.BlockSpec(memory_space=pltpu.HBM)


def per_device(positions, features, species, counts, species_energy, radial_weight, mix_weight, readout):
    energies, forces = pl.pallas_call(
        whole_kernel,
        out_shape=(
            jax.ShapeDtypeStruct((2, 2, 2, SLOTS), F32),
            jax.ShapeDtypeStruct((2, 2, 3, 2, SLOTS), F32),
        ),
        in_specs=[HBM] * 8,
        out_specs=(VMEM, VMEM),
        scratch_shapes=[
            pltpu.VMEM((2, 2, 3, 2, SLOTS), F32),
            pltpu.VMEM((2, 2, 2, SLOTS, LANES), F32),
            pltpu.VMEM((2, 2, 2, SLOTS), jnp.int32),
            pltpu.VMEM((2, 2, 2), jnp.int32),
            pltpu.SMEM(species_energy.shape, F32),
            pltpu.VMEM((3, BASIS, LANES), F32),
            pltpu.VMEM((3, LANES, LANES), F32),
            pltpu.VMEM((4, LANES), F32),
            pltpu.SemaphoreType.DMA((8,)),
            pltpu.VMEM((27, 8, LANES), F32),
            pltpu.VMEM((27, 2, 2, 2, SLOTS, LANES), F32),
            pltpu.SemaphoreType.DMA((2, 27)),
            pltpu.SemaphoreType.DMA((2, 27)),
            pltpu.VMEM((27, 8, LANES), F32),
            pltpu.SemaphoreType.DMA((27,)),
            pltpu.SemaphoreType.DMA((27,)),
            pltpu.VMEM((8, 8, NEAR), F32),
            pltpu.VMEM((LANES, LANES), F32),
            pltpu.VMEM((2 * LANES, 256), BF16),
            pltpu.VMEM((8, 2 * GHOST, 256), BF16),
            pltpu.VMEM((8, NEAR, 384), BF16),
            pltpu.VMEM((ROWS, 2 * LANES), BF16),
            pltpu.VMEM((ROWS, 2 * GHOST), BF16),
            pltpu.VMEM((ROWS, 256), F32),
            pltpu.VMEM((9, LANES, LANES), F32),
            pltpu.VMEM((8, 2 * BASIS, SLOTS, NEAR), F32),
            pltpu.VMEM((8, 4, SLOTS, NEAR), F32),
            pltpu.VMEM((ROWS, 384), BF16),
            pltpu.VMEM((ROWS, NEAR), F32),
            pltpu.VMEM((8, 8, NEAR), F32),
            pltpu.VMEM((3, LANES, LANES), F32),
            pltpu.VMEM((27, 8, LANES), F32),
        ],
        compiler_params=pltpu.CompilerParams(
            collective_id=0, has_side_effects=True, vmem_limit_bytes=60 * 2**20
        ),
    )(
        jnp.swapaxes(positions, 2, 3), features, species, counts, species_energy,
        jnp.swapaxes(radial_weight, 0, 1), mix_weight, readout,
    )
    return energies, jnp.swapaxes(forces, 2, 3)


def solution(mesh):
    grid = P("gx", "gy", "gz")
    return jax.shard_map(
        per_device,
        mesh=mesh,
        in_specs=(grid, grid, grid, grid, P(), P(), P(), P()),
        out_specs=(grid, grid),
        check_vma=False,
    )
```

time: 69.3 us -> 55.5 us (0.80)
  local copies, waits for them, and re-layouts: 8.65 us -> 1.88 us
  Pallas kernels: 59.5 us -> 52.8 us
    unnamed x19 -> x4, local copies, waits for them, and re-layouts: 8.65 us -> 1.88 us
    pallas_call x3 -> x1, Pallas kernels: 59.5 us -> 52.8 us  [per_device(): pl.pallas_call(whole_kernel, out_shape=(jax.ShapeDtypeStruct((2, 2, 2, SL...]
where the time goes in v2:
time: 55.5 us; the launch traced here: 55.3 us
  Pallas kernels  52.8 us (95%)
  local copies, waits for them, and re-layouts  1.88 us (3%)
  between operations  0.65 us (1%)
    pallas_call x1, Pallas kernels, per_device(): pl.pallas_call(whole_kernel, out_shape=(jax.ShapeDtypeStruct((2, 2, 2, SL...  52.8 us
    unnamed x4, local copies, waits for them, and re-layouts  1.88 us

profile of v2, /device:TPU:1, one launch (start us, length us, event | category | flops | bytes accessed | tf_op | source)
XLA Modules:
  0.0 55.3 jit_solution(15547978411702052305)
XLA Ops:
  0.6 52.8 %shard_map.95 = (f32[2,2,2,16]{3,2,1,0:T(2,128)}, f32[2,2,3,2,16]{4,3,2,1,0:T(2,128)}) custom-call(f32[2,2,3,2,16]{4,3,2,1,0:T(2,128)} %bitcast.3, f32[2,2,2,16,128]{4,3,2,1,0:T(8,128)} %feat_hbm.1, s32[2,2,2,16]{3,2,1,0:T(2,128)} %species_hbm.1, s32[2,2,2]{2,1,0:T(2,128)} %counts_hbm.1, f32[10]{0:T(128)} %table_hbm.1, f32[3,8,128]{2,1,0:T(8,128)} %bitcast.4, ...), custom_call_target="tpu_custom_call" | custom-call | tf_op jit(solution)/shard_map/pallas_call | solution.py:452
  53.4 0.0 copy-start
  53.4 1.3 %copy.12 = f32[2,2,2,16]{3,2,1,0:T(2,128)} copy(f32[2,2,2,16]{3,2,1,0:T(2,128)} %get-tuple-element.8) | data formatting | bytes 1024
  54.7 0.0 copy-done
  54.7 0.6 %copy.13 = f32[2,2,2,3,16]{4,2,3,1,0:T(2,128)} copy(f32[2,2,2,3,16]{4,2,3,1,0:T(2,128)S(1)} %bitcast.5) | data formatting | bytes 3072
Async XLA Ops:
  53.4 1.3 %copy-start = (f32[2,2,3,2,16]{4,3,2,1,0:T(2,128)S(1)}, f32[2,2,3,2,16]{4,3,2,1,0:T(2,128)}, u32[]{:S(2)}) copy-start(f32[2,2,3,2,16]{4,3,2,1,0:T(2,128)} %get-tuple-element.5) | copy-start | bytes 4612

commit v3 on v2

--- a/solution.py
+++ b/solution.py
@@ -89,6 +89,10 @@
     return tuple(place)
 
 
+def side(domain):
+    return OFFSETS[domain][0]
+
+
 def rim_of(domain):
     return tuple(
         pl.ds(0, 2) if step == 0 else pl.ds(1 if step == 1 else 0, 1) for step in OFFSETS[domain]
@@ -221,18 +225,115 @@
     npos[s, :, chunk * LANES : (chunk + 1) * LANES] = value
 
 
-def put_features(high, low, fcat, s, at, low_by, fback, back_at):
+def put_forward(high, low, fcat, at, low_by):
     rows, low_rows = slice(at, at + SLOTS), slice(at + low_by, at + low_by + SLOTS)
-    where = () if s is None else (s,)
-    fcat[where + (rows, slice(0, 128))] = high
-    fcat[where + (rows, slice(128, 256))] = low
-    fcat[where + (low_rows, slice(0, 128))] = high
-    fcat[where + (low_rows, slice(128, 256))] = jnp.zeros_like(low)
-    for b in range(8) if s is None else (s,):
-        rows = slice(back_at, back_at + SLOTS)
-        fback[b, rows, 0:128] = high
-        fback[b, rows, 128:256] = high
-        fback[b, rows, 256:384] = low
+    fcat[rows, 0:128] = high
+    fcat[rows, 128:256] = low
+    fcat[low_rows, 0:128] = high
+    fcat[low_rows, 128:256] = jnp.zeros_like(low)
+
+
+def put_backward(high, low, fback, at, low_by):
+    rows, low_rows = slice(at, at + SLOTS), slice(at + low_by, at + low_by + SLOTS)
+    fback[rows, 0:128] = high
+    fback[rows, 128:256] = high
+    fback[low_rows, 0:128] = low
+    fback[low_rows, 128:256] = jnp.zeros_like(low)
+
+
+def own_rows(s):
+    return pl.ds(pl.multiple_of(s * SLOTS, SLOTS), SLOTS)
+
+
+def over_cells(first, count, early, late):
+    def step(t, carry):
+        s = first + 2 * t
+        early(s, 0)
+        early(s + 1, 1)
+        late(s, 0)
+        late(s + 1, 1)
+        return carry
+
+    lax.fori_loop(0, count // 2, step, 0)
+
+
+def gradient_pairs(s, summed, radial, gpair):
+    for m in range(9):
+        slope = summed[m, own_rows(s), :]
+        l = DEGREE_OF[m]
+        for n in range(BASIS):
+            rows = slice((n * 9 + m) * SLOTS, (n * 9 + m + 1) * SLOTS)
+            high, low = halves(slope * radial[l, n : n + 1, :])
+            gpair[rows, 0:128] = high
+            gpair[rows, 128:256] = low
+
+
+def chunk_forces(s, chunk, dpair, high_at, low_at, geo, rad, ngrad):
+    at = slice(chunk * LANES, (chunk + 1) * LANES)
+    ux, uy, uz, inverse = (geo[s, a, :, at] for a in range(4))
+    harmonic = harmonics(ux, uy, uz)
+    amp = [None] * 9
+    along = None
+    for n in range(BASIS):
+        value, slope = rad[s, n, :, at], rad[s, BASIS + n, :, at]
+        inner = None
+        for m in range(9):
+            rows = slice((n * 9 + m) * SLOTS, (n * 9 + m + 1) * SLOTS)
+            part = dpair[rows, high_at : high_at + LANES] + dpair[rows, low_at : low_at + LANES]
+            if m > 0:
+                amp[m] = part * value if n == 0 else amp[m] + part * value
+            inner = part if m == 0 else inner + part * harmonic[m]
+        along = inner * slope if n == 0 else along + inner * slope
+    vx = R3 * amp[1] + R15 * (uy * amp[4] + uz * amp[7] + ux * amp[8]) - R5 * (ux * amp[6])
+    vy = R3 * amp[2] + R15 * (ux * amp[4] + uz * amp[5] - uy * amp[8]) - R5 * (uy * amp[6])
+    vz = R3 * amp[3] + R15 * (uy * amp[5] + ux * amp[7]) + (2.0 * R5) * (uz * amp[6])
+    central = along - inverse * (ux * vx + uy * vy + uz * vz)
+    slopes = [u * central + inverse * v for u, v in ((ux, vx), (uy, vy), (uz, vz))]
+    for a in range(3):
+        ngrad[s, a : a + 1, at] = jnp.sum(slopes[a], axis=0, keepdims=True)
+    return slopes
+
+
+def scatter(s, chunk, ngrad, grads):
+    whole = ngrad[s, :, chunk * LANES : (chunk + 1) * LANES]
+    for (domain, turn), places in grouped(TABLES[s], chunk):
+        piece = whole if len(places) == 8 else jnp.where(places_mask(places), whole, 0.0)
+        if turn:
+            piece = pltpu.roll(piece, (8 - turn) * SLOTS, 1)
+        grads[domain] = grads[domain] + piece
+
+
+SPANS = (slice(0, 1), slice(1, 4), slice(4, 9))
+
+
+def mix_half(half, slot, counts, mix, readout, summed, layers):
+    rows = slice(half * 64, (half + 1) * 64)
+    occupied = jnp.concatenate(
+        [
+            jnp.where(slot < counts[half, y : y + 1, z : z + 1], 1.0, 0.0)
+            for y in (0, 1)
+            for z in (0, 1)
+        ],
+        axis=0,
+    )
+    mixed = []
+    for l, span in enumerate(SPANS):
+        size = span.stop - span.start
+        part = dot_split(summed[span, rows].reshape(size * 64, LANES), mix[l])
+        mixed += [part[i * 64 : (i + 1) * 64] for i in range(size)]
+    q0 = mixed[0]
+    q1 = sum(v * v for v in mixed[1:4])
+    q2 = sum(v * v for v in mixed[4:9])
+    r0, r1, r2, r3 = (readout[i : i + 1, :] for i in range(4))
+    layers[rows] = q0 * r0 + q1 * r1 + q2 * r2 + (q0 * q1) * r3
+    slope1 = 2.0 * occupied * (r1 + q0 * r3)
+    slope2 = 2.0 * occupied * r2
+    back = [occupied * (r0 + q1 * r3)]
+    back += [v * slope1 for v in mixed[1:4]]
+    back += [v * slope2 for v in mixed[4:9]]
+    for l, span in enumerate(SPANS):
+        part = dot_split(jnp.concatenate(back[span], axis=0), mix[l], 1)
+        summed[span, rows] = part.reshape(span.stop - span.start, 64, LANES)
 
 
 def whole_kernel(
@@ -240,9 +341,12 @@
     energy_ref, force_ref,
     pos, feat, species, counts, table, radial, mix, readout, loads,
     tiles, feats, sends, recvs, landed, back_sends, back_recvs,
-    npos, post, fown, fcat, fback, opair, pair, mom, summed, rad, geo, gpair, dpair, ngrad, center,
-    grads,
+    npos, post, fown, fcat, bown, bcat, opair0, opair1, pair0, pair1, mom0, mom1,
+    summed, layers, rad, geo, gpair0, gpair1, odpair0, odpair1, dpair0, dpair1,
+    ngrad, center, grads,
 ):
+    opair, pair, mom = (opair0, opair1), (pair0, pair1), (mom0, mom1)
+    gpair, odpair, dpair = (gpair0, gpair1), (odpair0, odpair1), (dpair0, dpair1)
     barrier = greet()
     held = [
         pltpu.make_async_copy(source, target, loads.at[i])
@@ -270,26 +374,27 @@
     shift = jnp.where(row == 0, lane // 64, jnp.where(row == 1, lane // 32 % 2, lane // 16 % 2))
     tiles[SELF] = tiles[SELF] + CELL_SIDE * shift.astype(F32)
 
-    copies = []
+    halo = {}
     for domain in range(27):
         if domain == SELF:
             continue
         there, rim, back = neighbour(domain), rim_of(domain), 26 - domain
-        copies.append(
+        halo[domain] = (
             pltpu.make_async_remote_copy(
                 tiles.at[SELF], tiles.at[back], sends.at[0, domain], recvs.at[0, back],
                 device_id=there, device_id_type=MESH,
-            )
-        )
-        copies.append(
+            ),
             pltpu.make_async_remote_copy(
                 feats.at[(SELF,) + rim], feats.at[(back,) + rim], sends.at[1, domain],
                 recvs.at[1, back], device_id=there, device_id_type=MESH,
-            )
+            ),
         )
     pl.semaphore_wait(barrier, 26)
-    for copy in copies:
-        copy.start()
+    for step in (-1, 0, 1):
+        for domain, pieces in halo.items():
+            if side(domain) == step:
+                for copy in pieces:
+                    copy.start()
 
     for s in range(8):
         put_near(s, 0, npos, tiles)
@@ -297,151 +402,116 @@
     post[...] = jnp.transpose(jnp.concatenate([mine] * 16, axis=0))
     for q, (x, y, z) in enumerate(CELLS):
         high, low = halves(feats[SELF, x, y, z])
-        put_features(high, low, fown, None, q * SLOTS, LANES, fback, q * SLOTS)
+        put_forward(high, low, fown, q * SLOTS, LANES)
+        put_backward(high, low, bown, q * SLOTS, LANES)
     for copy in held[3:]:
         copy.wait()
 
-    def inside(s, carry):
-        near_pairs(s, 0, npos, post, geo, rad, opair, 0, LANES)
-        mom[...] = dot(opair[...], fown[...])
-        own = pl.ds(pl.multiple_of(s * SLOTS, SLOTS), SLOTS)
+    def own_pairs(s, b):
+        near_pairs(s, 0, npos, post, geo, rad, opair[b], 0, LANES)
+
+    def own_moments(s, b):
+        mom[b][...] = dot(opair[b][...], fown[...])
         for m in range(9):
-            summed[m, own, :] = weighted(mom, radial, m)
-        return carry
-
-    lax.fori_loop(0, 8, inside, 0)
-
-    for copy in copies:
-        copy.wait()
-    for s in range(8):
-        for chunk in range(1, CHUNKS):
-            put_near(s, chunk, npos, tiles)
-        filled = {(c, p): (domain, q) for c, p, domain, q in TABLES[s]}
-        for chunk in range(1, CHUNKS):
-            for place in range(8):
-                at = (chunk - 1) * LANES + place * SLOTS
-                if (chunk, place) in filled:
-                    domain, q = filled[(chunk, place)]
-                    high, low = halves(feats[(domain,) + CELLS[q]])
-                else:
-                    high = low = jnp.zeros((SLOTS, LANES), BF16)
-                put_features(high, low, fcat, s, at, GHOST, fback, at + LANES)
-
-    def outside(s, carry):
+            summed[m, own_rows(s), :] = weighted(mom[b], radial, m)
+
+    over_cells(0, 8, own_pairs, own_moments)
+
+    def ghost_pairs(s, b):
         for chunk in range(1, CHUNKS):
             at = (chunk - 1) * LANES
-            near_pairs(s, chunk, npos, post, geo, rad, pair, at, GHOST + at)
-        mom[...] = dot(pair[...], fcat[s])
-        own = pl.ds(pl.multiple_of(s * SLOTS, SLOTS), SLOTS)
+            near_pairs(s, chunk, npos, post, geo, rad, pair[b], at, GHOST + at)
+
+    def ghost_moments(s, b):
+        mom[b][...] = dot(pair[b][...], fcat[s])
         for m in range(9):
-            summed[m, own, :] = summed[m, own, :] + weighted(mom, radial, m)
-        return carry
-
-    lax.fori_loop(0, 8, outside, 0)
-
-    occupied = jnp.concatenate(
-        [jnp.where(slot < counts[x, y : y + 1, z : z + 1], 1.0, 0.0) for x, y, z in CELLS], axis=0
-    )
-    mixed = []
-    for l, span in enumerate((slice(0, 1), slice(1, 4), slice(4, 9))):
-        part = summed[span].reshape((span.stop - span.start) * LANES, LANES)
-        part = dot_split(part, mix[l])
-        mixed += [part[i * LANES : (i + 1) * LANES] for i in range(span.stop - span.start)]
-    q0 = mixed[0]
-    q1 = sum(v * v for v in mixed[1:4])
-    q2 = sum(v * v for v in mixed[4:9])
-    r0, r1, r2, r3 = (readout[i : i + 1, :] for i in range(4))
-    layer = q0 * r0 + q1 * r1 + q2 * r2 + (q0 * q1) * r3
-    layer = jnp.sum(jnp.transpose(layer), axis=0, keepdims=True)
+            summed[m, own_rows(s), :] = summed[m, own_rows(s), :] + weighted(mom[b], radial, m)
+
+    def ghost_gradients(s, b):
+        gradient_pairs(s, summed, radial, gpair[b])
+        dpair[b][...] = dot(gpair[b][...], bcat[s], 1)
+
+    def ghost_forces(s, b):
+        pull = None
+        for chunk in range(1, CHUNKS):
+            at = (chunk - 1) * LANES
+            more = chunk_forces(s, chunk, dpair[b], at, GHOST + at, geo, rad, ngrad)
+            pull = more if pull is None else [p + q for p, q in zip(pull, more)]
+        for a in range(3):
+            center[a, own_rows(s), :] = pull[a]
+
+    returns = {
+        domain: pltpu.make_async_remote_copy(
+            grads.at[domain], landed.at[26 - domain], back_sends.at[domain],
+            back_recvs.at[26 - domain], device_id=neighbour(domain), device_id_type=MESH,
+        )
+        for domain in range(27)
+        if domain != SELF
+    }
+    for half in (1, 0):
+        for domain, pieces in halo.items():
+            if (side(domain) == 1) == (half == 0):
+                for copy in pieces:
+                    copy.wait_recv()
+        for s in range(4 * half, 4 * half + 4):
+            for chunk in range(1, CHUNKS):
+                put_near(s, chunk, npos, tiles)
+            filled = {(c, p): (domain, q) for c, p, domain, q in TABLES[s]}
+            for chunk in range(1, CHUNKS):
+                for place in range(8):
+                    at = (chunk - 1) * LANES + place * SLOTS
+                    if (chunk, place) in filled:
+                        domain, q = filled[(chunk, place)]
+                        high, low = halves(feats[(domain,) + CELLS[q]])
+                    else:
+                        high = low = jnp.zeros((SLOTS, LANES), BF16)
+                    put_forward(high, low, fcat.at[s], at, GHOST)
+                    put_backward(high, low, bcat.at[s], at, GHOST)
+        over_cells(4 * half, 4, ghost_pairs, ghost_moments)
+        mix_half(half, slot, counts, mix, readout, summed, layers)
+        over_cells(4 * half, 4, ghost_gradients, ghost_forces)
+        for s in range(4 * half, 4 * half + 4):
+            for chunk in range(1, CHUNKS):
+                scatter(s, chunk, ngrad, grads)
+        for domain, copy in returns.items():
+            if (side(domain) == 1) == (half == 1):
+                copy.start()
+
+    def own_gradients(s, b):
+        gradient_pairs(s, summed, radial, gpair[b])
+        odpair[b][...] = dot(gpair[b][...], bown[...], 1)
+
+    def own_forces(s, b):
+        pull = chunk_forces(s, 0, odpair[b], 0, LANES, geo, rad, ngrad)
+        for a in range(3):
+            center[a, own_rows(s), :] = center[a, own_rows(s), :] + pull[a]
+
+    over_cells(0, 8, own_gradients, own_forces)
+    for s in range(8):
+        scatter(s, 0, ngrad, grads)
+    total = grads[SELF]
+    pulls = [jnp.sum(jnp.transpose(center[a]), axis=0, keepdims=True) for a in range(3)]
+    total = total - jnp.concatenate(pulls + [jnp.zeros((5, LANES), F32)], axis=0)
+
+    layer = jnp.sum(jnp.transpose(layers[...]), axis=0, keepdims=True)
     lane16 = lax.broadcasted_iota(jnp.int32, (1, SLOTS), 1)
     for q, (x, y, z) in enumerate(CELLS):
         kind = species[x, y, z : z + 1, :]
         value = layer[:, q * SLOTS : (q + 1) * SLOTS]
         for k in range(table.shape[0]):
             value = value + jnp.where(kind == k, table[k], 0.0)
-        energy_ref[x, y, z : z + 1, :] = jnp.where(lane16 < counts[x, y : y + 1, z : z + 1], value, 0.0)
-    slope1 = 2.0 * occupied * (r1 + q0 * r3)
-    slope2 = 2.0 * occupied * r2
-    back = [occupied * (r0 + q1 * r3)]
-    back += [v * slope1 for v in mixed[1:4]]
-    back += [v * slope2 for v in mixed[4:9]]
-    for l, span in enumerate((slice(0, 1), slice(1, 4), slice(4, 9))):
-        part = dot_split(jnp.concatenate(back[span], axis=0), mix[l], 1)
-        summed[span] = part.reshape(span.stop - span.start, LANES, LANES)
-
-    def backward(s, carry):
-        own = pl.ds(pl.multiple_of(s * SLOTS, SLOTS), SLOTS)
-        for m in range(9):
-            slope = summed[m, own, :]
-            l = DEGREE_OF[m]
-            for n in range(BASIS):
-                rows = slice((n * 9 + m) * SLOTS, (n * 9 + m + 1) * SLOTS)
-                high, low = halves(slope * radial[l, n : n + 1, :])
-                gpair[rows, 0:128] = high
-                gpair[rows, 128:256] = low
-                gpair[rows, 256:384] = high
-        dpair[...] = dot(gpair[...], fback[s], 1)
-        pull = [None] * 3
-        for chunk in range(CHUNKS):
-            at = slice(chunk * LANES, (chunk + 1) * LANES)
-            ux, uy, uz, inverse = (geo[s, a, :, at] for a in range(4))
-            harmonic = harmonics(ux, uy, uz)
-            amp = [None] * 9
-            along = None
-            for n in range(BASIS):
-                value, slope = rad[s, n, :, at], rad[s, BASIS + n, :, at]
-                inner = None
-                for m in range(9):
-                    part = dpair[(n * 9 + m) * SLOTS : (n * 9 + m + 1) * SLOTS, at]
-                    if m > 0:
-                        amp[m] = part * value if n == 0 else amp[m] + part * value
-                    inner = part if m == 0 else inner + part * harmonic[m]
-                along = inner * slope if n == 0 else along + inner * slope
-            vx = R3 * amp[1] + R15 * (uy * amp[4] + uz * amp[7] + ux * amp[8]) - R5 * (ux * amp[6])
-            vy = R3 * amp[2] + R15 * (ux * amp[4] + uz * amp[5] - uy * amp[8]) - R5 * (uy * amp[6])
-            vz = R3 * amp[3] + R15 * (uy * amp[5] + ux * amp[7]) + (2.0 * R5) * (uz * amp[6])
-            central = along - inverse * (ux * vx + uy * vy + uz * vz)
-            for a, (u, v) in enumerate(((ux, vx), (uy, vy), (uz, vz))):
-                slope = u * central + inverse * v
-                ngrad[s, a : a + 1, at] = jnp.sum(slope, axis=0, keepdims=True)
-                pull[a] = slope if chunk == 0 else pull[a] + slope
-        for a in range(3):
-            center[a, own, :] = pull[a]
-        return carry
-
-    lax.fori_loop(0, 8, backward, 0)
-
-    for a in range(3):
-        grads[SELF, a : a + 1, :] = -jnp.sum(jnp.transpose(center[a]), axis=0, keepdims=True)
-    for s in range(8):
-        for chunk in range(CHUNKS):
-            whole = ngrad[s, :, chunk * LANES : (chunk + 1) * LANES]
-            for (domain, turn), places in grouped(TABLES[s], chunk):
-                piece = whole if len(places) == 8 else jnp.where(places_mask(places), whole, 0.0)
-                if turn:
-                    piece = pltpu.roll(piece, (8 - turn) * SLOTS, 1)
-                grads[domain] = grads[domain] + piece
-
-    copies = []
-    for domain in range(27):
-        if domain != SELF:
-            copies.append(
-                pltpu.make_async_remote_copy(
-                    grads.at[domain], landed.at[26 - domain], back_sends.at[domain],
-                    back_recvs.at[26 - domain], device_id=neighbour(domain), device_id_type=MESH,
-                )
-            )
-    for copy in copies:
-        copy.start()
-    for copy in copies:
-        copy.wait()
-    total = grads[SELF]
-    for domain in range(27):
-        if domain != SELF:
-            total = total + landed[domain]
+        occupied = lane16 < counts[x, y : y + 1, z : z + 1]
+        energy_ref[x, y, z : z + 1, :] = jnp.where(occupied, value, 0.0)
+
+    for domain, copy in returns.items():
+        copy.wait_recv()
+        total = total + landed[26 - domain]
     total = -total
     for q, (x, y, z) in enumerate(CELLS):
         force_ref[x, y, :, z, :] = total[0:3, q * SLOTS : (q + 1) * SLOTS]
+    for domain, pieces in halo.items():
+        for copy in pieces + (returns[domain],):
+            copy.wait_send()
 
 
 VMEM = pl.BlockSpec(memory_space=pltpu.VMEM)
@@ -478,15 +548,24 @@
             pltpu.VMEM((LANES, LANES), F32),
             pltpu.VMEM((2 * LANES, 256), BF16),
             pltpu.VMEM((8, 2 * GHOST, 256), BF16),
-            pltpu.VMEM((8, NEAR, 384), BF16),
+            pltpu.VMEM((2 * LANES, 256), BF16),
+            pltpu.VMEM((8, 2 * GHOST, 256), BF16),
+            pltpu.VMEM((ROWS, 2 * LANES), BF16),
             pltpu.VMEM((ROWS, 2 * LANES), BF16),
             pltpu.VMEM((ROWS, 2 * GHOST), BF16),
+            pltpu.VMEM((ROWS, 2 * GHOST), BF16),
+            pltpu.VMEM((ROWS, 256), F32),
             pltpu.VMEM((ROWS, 256), F32),
             pltpu.VMEM((9, LANES, LANES), F32),
+            pltpu.VMEM((LANES, LANES), F32),
             pltpu.VMEM((8, 2 * BASIS, SLOTS, NEAR), F32),
             pltpu.VMEM((8, 4, SLOTS, NEAR), F32),
-            pltpu.VMEM((ROWS, 384), BF16),
-            pltpu.VMEM((ROWS, NEAR), F32),
+            pltpu.VMEM((ROWS, 256), BF16),
+            pltpu.VMEM((ROWS, 256), BF16),
+            pltpu.VMEM((ROWS, 2 * LANES), F32),
+            pltpu.VMEM((ROWS, 2 * LANES), F32),
+            pltpu.VMEM((ROWS, 2 * GHOST), F32),
+            pltpu.VMEM((ROWS, 2 * GHOST), F32),
             pltpu.VMEM((8, 8, NEAR), F32),
             pltpu.VMEM((3, LANES, LANES), F32),
             pltpu.VMEM((27, 8, LANES), F32),

time: 55.5 us -> 50 us (0.901)
  Pallas kernels: 52.8 us -> 47.2 us
    pallas_call x1, Pallas kernels: 52.8 us -> 47.2 us  [per_device(): pl.pallas_call(whole_kernel, out_shape=(jax.ShapeDtypeStruct((2, 2, 2, SL...]
where the time goes in v3:
time: 50 us; the launch traced here: 49.8 us
  Pallas kernels  47.2 us (94%)
  local copies, waits for them, and re-layouts  1.88 us (4%)
  between operations  0.65 us (1%)
    pallas_call x1, Pallas kernels, per_device(): pl.pallas_call(whole_kernel, out_shape=(jax.ShapeDtypeStruct((2, 2, 2, SL...  47.2 us
    unnamed x4, local copies, waits for them, and re-layouts  1.88 us

profile of v3, /device:TPU:1, one launch (start us, length us, event | category | flops | bytes accessed | tf_op | source)
XLA Modules:
  0.0 49.8 jit_solution(18115242312175858473)
XLA Ops:
  0.6 47.2 %shard_map.95 = (f32[2,2,2,16]{3,2,1,0:T(2,128)}, f32[2,2,3,2,16]{4,3,2,1,0:T(2,128)}) custom-call(f32[2,2,3,2,16]{4,3,2,1,0:T(2,128)} %bitcast.3, f32[2,2,2,16,128]{4,3,2,1,0:T(8,128)} %feat_hbm.1, s32[2,2,2,16]{3,2,1,0:T(2,128)} %species_hbm.1, s32[2,2,2]{2,1,0:T(2,128)} %counts_hbm.1, f32[10]{0:T(128)} %table_hbm.1, f32[3,8,128]{2,1,0:T(8,128)} %bitcast.4, ...), custom_call_target="tpu_custom_call" | custom-call | tf_op jit(solution)/shard_map/pallas_call | solution.py:522
  47.9 0.0 copy-start
  47.9 1.3 %copy.12 = f32[2,2,2,16]{3,2,1,0:T(2,128)} copy(f32[2,2,2,16]{3,2,1,0:T(2,128)} %get-tuple-element.8) | data formatting | bytes 1024
  49.2 0.0 copy-done
  49.2 0.6 %copy.13 = f32[2,2,2,3,16]{4,2,3,1,0:T(2,128)} copy(f32[2,2,2,3,16]{4,2,3,1,0:T(2,128)S(1)} %bitcast.5) | data formatting | bytes 3072
Async XLA Ops:
  47.9 1.3 %copy-start = (f32[2,2,3,2,16]{4,3,2,1,0:T(2,128)S(1)}, f32[2,2,3,2,16]{4,3,2,1,0:T(2,128)}, u32[]{:S(2)}) copy-start(f32[2,2,3,2,16]{4,3,2,1,0:T(2,128)} %get-tuple-element.5) | copy-start | bytes 4612

commit v4 on v3

--- a/solution.py
+++ b/solution.py
@@ -17,6 +17,7 @@
 CHUNKS = 4
 NEAR = CHUNKS * LANES
 GHOST = NEAR - LANES
+STEP = 4
 ROWS = BASIS * 9 * SLOTS
 DEGREE_OF = (0, 1, 1, 1, 2, 2, 2, 2, 2)
 SELF = 13
@@ -247,14 +248,14 @@
 
 def over_cells(first, count, early, late):
     def step(t, carry):
-        s = first + 2 * t
-        early(s, 0)
-        early(s + 1, 1)
-        late(s, 0)
-        late(s + 1, 1)
+        s = first + STEP * t
+        for b in range(STEP):
+            early(s + b, b)
+        for b in range(STEP):
+            late(s + b, b)
         return carry
 
-    lax.fori_loop(0, count // 2, step, 0)
+    lax.fori_loop(0, count // STEP, step, 0)
 
 
 def gradient_pairs(s, summed, radial, gpair):
@@ -341,12 +342,12 @@
     energy_ref, force_ref,
     pos, feat, species, counts, table, radial, mix, readout, loads,
     tiles, feats, sends, recvs, landed, back_sends, back_recvs,
-    npos, post, fown, fcat, bown, bcat, opair0, opair1, pair0, pair1, mom0, mom1,
-    summed, layers, rad, geo, gpair0, gpair1, odpair0, odpair1, dpair0, dpair1,
-    ngrad, center, grads,
+    npos, post, fown, fcat, bown, bcat, summed, layers, rad, geo, ngrad, center, grads,
+    *buffers,
 ):
-    opair, pair, mom = (opair0, opair1), (pair0, pair1), (mom0, mom1)
-    gpair, odpair, dpair = (gpair0, gpair1), (odpair0, odpair1), (dpair0, dpair1)
+    opair, pair, mom, gpair, odpair, dpair = (
+        buffers[i * STEP : (i + 1) * STEP] for i in range(6)
+    )
     barrier = greet()
     held = [
         pltpu.make_async_copy(source, target, loads.at[i])
@@ -389,12 +390,18 @@
                 recvs.at[1, back], device_id=there, device_id_type=MESH,
             ),
         )
-    pl.semaphore_wait(barrier, 26)
-    for step in (-1, 0, 1):
-        for domain, pieces in halo.items():
-            if side(domain) == step:
-                for copy in pieces:
-                    copy.start()
+
+    def send_halo():
+        pl.semaphore_wait(barrier, 26)
+        for step in (-1, 0, 1):
+            for domain, pieces in halo.items():
+                if side(domain) == step:
+                    for copy in pieces:
+                        copy.start()
+
+    planes = max(lax.axis_size("gx") // 2, 1)
+    early = lax.rem(lax.axis_index("gx"), planes) == 0
+    pl.when(jnp.logical_not(early))(send_halo)
 
     for s in range(8):
         put_near(s, 0, npos, tiles)
@@ -416,6 +423,7 @@
             summed[m, own_rows(s), :] = weighted(mom[b], radial, m)
 
     over_cells(0, 8, own_pairs, own_moments)
+    pl.when(early)(send_halo)
 
     def ghost_pairs(s, b):
         for chunk in range(1, CHUNKS):
@@ -550,25 +558,19 @@
             pltpu.VMEM((8, 2 * GHOST, 256), BF16),
             pltpu.VMEM((2 * LANES, 256), BF16),
             pltpu.VMEM((8, 2 * GHOST, 256), BF16),
-            pltpu.VMEM((ROWS, 2 * LANES), BF16),
-            pltpu.VMEM((ROWS, 2 * LANES), BF16),
-            pltpu.VMEM((ROWS, 2 * GHOST), BF16),
-            pltpu.VMEM((ROWS, 2 * GHOST), BF16),
-            pltpu.VMEM((ROWS, 256), F32),
-            pltpu.VMEM((ROWS, 256), F32),
             pltpu.VMEM((9, LANES, LANES), F32),
             pltpu.VMEM((LANES, LANES), F32),
             pltpu.VMEM((8, 2 * BASIS, SLOTS, NEAR), F32),
             pltpu.VMEM((8, 4, SLOTS, NEAR), F32),
-            pltpu.VMEM((ROWS, 256), BF16),
-            pltpu.VMEM((ROWS, 256), BF16),
-            pltpu.VMEM((ROWS, 2 * LANES), F32),
-            pltpu.VMEM((ROWS, 2 * LANES), F32),
-            pltpu.VMEM((ROWS, 2 * GHOST), F32),
-            pltpu.VMEM((ROWS, 2 * GHOST), F32),
             pltpu.VMEM((8, 8, NEAR), F32),
             pltpu.VMEM((3, LANES, LANES), F32),
             pltpu.VMEM((27, 8, LANES), F32),
+            *[pltpu.VMEM((ROWS, 2 * LANES), BF16)] * STEP,
+            *[pltpu.VMEM((ROWS, 2 * GHOST), BF16)] * STEP,
+            *[pltpu.VMEM((ROWS, 256), F32)] * STEP,
+            *[pltpu.VMEM((ROWS, 256), BF16)] * STEP,
+            *[pltpu.VMEM((ROWS, 2 * LANES), F32)] * STEP,
+            *[pltpu.VMEM((ROWS, 2 * GHOST), F32)] * STEP,
         ],
         compiler_params=pltpu.CompilerParams(
             collective_id=0, has_side_effects=True, vmem_limit_bytes=60 * 2**20

time: 50 us -> 48.5 us (0.970)
  Pallas kernels: 47.2 us -> 45.8 us
    pallas_call x1, Pallas kernels: 47.2 us -> 45.8 us  [per_device(): pl.pallas_call(whole_kernel, out_shape=(jax.ShapeDtypeStruct((2, 2, 2, SL...]
where the time goes in v4:
time: 48.5 us; the launch traced here: 48.3 us
  Pallas kernels  45.8 us (94%)
  local copies, waits for them, and re-layouts  1.88 us (4%)
  between operations  0.65 us (1%)
    pallas_call x1, Pallas kernels, per_device(): pl.pallas_call(whole_kernel, out_shape=(jax.ShapeDtypeStruct((2, 2, 2, SL...  45.8 us
    unnamed x4, local copies, waits for them, and re-layouts  1.88 us

profile of v4, /device:TPU:1, one launch (start us, length us, event | category | flops | bytes accessed | tf_op | source)
XLA Modules:
  0.0 48.3 jit_solution(15427741215519334187)
XLA Ops:
  0.6 45.8 %shard_map.95 = (f32[2,2,2,16]{3,2,1,0:T(2,128)}, f32[2,2,3,2,16]{4,3,2,1,0:T(2,128)}) custom-call(f32[2,2,3,2,16]{4,3,2,1,0:T(2,128)} %bitcast.3, f32[2,2,2,16,128]{4,3,2,1,0:T(8,128)} %feat_hbm.1, s32[2,2,2,16]{3,2,1,0:T(2,128)} %species_hbm.1, s32[2,2,2]{2,1,0:T(2,128)} %counts_hbm.1, f32[10]{0:T(128)} %table_hbm.1, f32[3,8,128]{2,1,0:T(8,128)} %bitcast.4, ...), custom_call_target="tpu_custom_call" | custom-call | tf_op jit(solution)/shard_map/pallas_call | solution.py:530
  46.4 0.0 copy-start
  46.4 1.3 %copy.12 = f32[2,2,2,16]{3,2,1,0:T(2,128)} copy(f32[2,2,2,16]{3,2,1,0:T(2,128)} %get-tuple-element.8) | data formatting | bytes 1024
  47.7 0.0 copy-done
  47.7 0.6 %copy.13 = f32[2,2,2,3,16]{4,2,3,1,0:T(2,128)} copy(f32[2,2,2,3,16]{4,2,3,1,0:T(2,128)S(1)} %bitcast.5) | data formatting | bytes 3072
Async XLA Ops:
  46.4 1.3 %copy-start = (f32[2,2,3,2,16]{4,3,2,1,0:T(2,128)S(1)}, f32[2,2,3,2,16]{4,3,2,1,0:T(2,128)}, u32[]{:S(2)}) copy-start(f32[2,2,3,2,16]{4,3,2,1,0:T(2,128)} %get-tuple-element.5) | copy-start | bytes 4612

commit v5 on v4

--- a/solution.py
+++ b/solution.py
@@ -18,6 +18,7 @@
 NEAR = CHUNKS * LANES
 GHOST = NEAR - LANES
 STEP = 4
+TILE = 4
 ROWS = BASIS * 9 * SLOTS
 DEGREE_OF = (0, 1, 1, 1, 2, 2, 2, 2, 2)
 SELF = 13
@@ -74,7 +75,7 @@
 
 
 def places_mask(places):
-    lane = lax.broadcasted_iota(jnp.int32, (8, LANES), 1)
+    lane = lax.broadcasted_iota(jnp.int32, (TILE, LANES), 1)
     mask = None
     for place in places:
         one = (lane >= place * SLOTS) & (lane < (place + 1) * SLOTS)
@@ -213,8 +214,8 @@
 
 
 def put_near(s, chunk, npos, tiles):
-    row = lax.broadcasted_iota(jnp.int32, (8, LANES), 0)
-    value = jnp.full((8, LANES), 100.0, F32)
+    row = lax.broadcasted_iota(jnp.int32, (TILE, LANES), 0)
+    value = jnp.full((TILE, LANES), 100.0, F32)
     for (domain, turn), places in grouped(TABLES[s], chunk):
         ox, oy, oz = (2.0 * CELL_SIDE * o for o in OFFSETS[domain])
         piece = tiles[domain]
@@ -246,13 +247,12 @@
     return pl.ds(pl.multiple_of(s * SLOTS, SLOTS), SLOTS)
 
 
-def over_cells(first, count, early, late):
+def over_cells(first, count, *works):
     def step(t, carry):
         s = first + STEP * t
-        for b in range(STEP):
-            early(s + b, b)
-        for b in range(STEP):
-            late(s + b, b)
+        for work in works:
+            for b in range(STEP):
+                work(s + b, b)
         return carry
 
     lax.fori_loop(0, count // STEP, step, 0)
@@ -361,7 +361,7 @@
     for copy in held:
         copy.start()
     slot = lax.broadcasted_iota(jnp.int32, (SLOTS, LANES), 0)
-    tiles[SELF] = jnp.zeros((8, LANES), F32)
+    tiles[SELF] = jnp.zeros((TILE, LANES), F32)
     ngrad[...] = jnp.zeros_like(ngrad)
     grads[...] = jnp.zeros_like(grads)
     for copy in held[:3]:
@@ -370,8 +370,8 @@
         tiles[SELF, 0:3, q * SLOTS : (q + 1) * SLOTS] = pos[x, y, :, z, :]
         occupied = slot < counts[x, y : y + 1, z : z + 1]
         feats[SELF, x, y, z] = jnp.where(occupied, feat[x, y, z], 0.0)
-    lane = lax.broadcasted_iota(jnp.int32, (8, LANES), 1)
-    row = lax.broadcasted_iota(jnp.int32, (8, LANES), 0)
+    lane = lax.broadcasted_iota(jnp.int32, (TILE, LANES), 1)
+    row = lax.broadcasted_iota(jnp.int32, (TILE, LANES), 0)
     shift = jnp.where(row == 0, lane // 64, jnp.where(row == 1, lane // 32 % 2, lane // 16 % 2))
     tiles[SELF] = tiles[SELF] + CELL_SIDE * shift.astype(F32)
 
@@ -393,11 +393,11 @@
 
     def send_halo():
         pl.semaphore_wait(barrier, 26)
-        for step in (-1, 0, 1):
-            for domain, pieces in halo.items():
-                if side(domain) == step:
-                    for copy in pieces:
-                        copy.start()
+        for piece in (0, 1):
+            for step in (-1, 0, 1):
+                for domain, pieces in halo.items():
+                    if side(domain) == step:
+                        pieces[piece].start()
 
     planes = max(lax.axis_size("gx") // 2, 1)
     early = lax.rem(lax.axis_index("gx"), planes) == 0
@@ -406,7 +406,7 @@
     for s in range(8):
         put_near(s, 0, npos, tiles)
     mine = tiles[SELF]
-    post[...] = jnp.transpose(jnp.concatenate([mine] * 16, axis=0))
+    post[...] = jnp.transpose(jnp.concatenate([mine] * (LANES // TILE), axis=0))
     for q, (x, y, z) in enumerate(CELLS):
         high, low = halves(feats[SELF, x, y, z])
         put_forward(high, low, fown, q * SLOTS, LANES)
@@ -457,13 +457,19 @@
         if domain != SELF
     }
     for half in (1, 0):
-        for domain, pieces in halo.items():
-            if (side(domain) == 1) == (half == 0):
-                for copy in pieces:
-                    copy.wait_recv()
+        coming = [
+            pieces for domain, pieces in halo.items() if (side(domain) == 1) == (half == 0)
+        ]
+        for positions, _ in coming:
+            positions.wait_recv()
         for s in range(4 * half, 4 * half + 4):
             for chunk in range(1, CHUNKS):
                 put_near(s, chunk, npos, tiles)
+        if half == 1:
+            over_cells(4, 4, ghost_pairs)
+        for _, features in coming:
+            features.wait_recv()
+        for s in range(4 * half, 4 * half + 4):
             filled = {(c, p): (domain, q) for c, p, domain, q in TABLES[s]}
             for chunk in range(1, CHUNKS):
                 for place in range(8):
@@ -475,7 +481,10 @@
                         high = low = jnp.zeros((SLOTS, LANES), BF16)
                     put_forward(high, low, fcat.at[s], at, GHOST)
                     put_backward(high, low, bcat.at[s], at, GHOST)
-        over_cells(4 * half, 4, ghost_pairs, ghost_moments)
+        if half == 1:
+            over_cells(4, 4, ghost_moments)
+        else:
+            over_cells(0, 4, ghost_pairs, ghost_moments)
         mix_half(half, slot, counts, mix, readout, summed, layers)
         over_cells(4 * half, 4, ghost_gradients, ghost_forces)
         for s in range(4 * half, 4 * half + 4):
@@ -499,7 +508,7 @@
         scatter(s, 0, ngrad, grads)
     total = grads[SELF]
     pulls = [jnp.sum(jnp.transpose(center[a]), axis=0, keepdims=True) for a in range(3)]
-    total = total - jnp.concatenate(pulls + [jnp.zeros((5, LANES), F32)], axis=0)
+    total = total - jnp.concatenate(pulls + [jnp.zeros((TILE - 3, LANES), F32)], axis=0)
 
     layer = jnp.sum(jnp.transpose(layers[...]), axis=0, keepdims=True)
     lane16 = lax.broadcasted_iota(jnp.int32, (1, SLOTS), 1)
@@ -545,14 +554,14 @@
             pltpu.VMEM((3, LANES, LANES), F32),
             pltpu.VMEM((4, LANES), F32),
             pltpu.SemaphoreType.DMA((8,)),
-            pltpu.VMEM((27, 8, LANES), F32),
+            pltpu.VMEM((27, TILE, LANES), F32),
             pltpu.VMEM((27, 2, 2, 2, SLOTS, LANES), F32),
             pltpu.SemaphoreType.DMA((2, 27)),
             pltpu.SemaphoreType.DMA((2, 27)),
-            pltpu.VMEM((27, 8, LANES), F32),
+            pltpu.VMEM((27, TILE, LANES), F32),
             pltpu.SemaphoreType.DMA((27,)),
             pltpu.SemaphoreType.DMA((27,)),
-            pltpu.VMEM((8, 8, NEAR), F32),
+            pltpu.VMEM((8, TILE, NEAR), F32),
             pltpu.VMEM((LANES, LANES), F32),
             pltpu.VMEM((2 * LANES, 256), BF16),
             pltpu.VMEM((8, 2 * GHOST, 256), BF16),
@@ -562,9 +571,9 @@
             pltpu.VMEM((LANES, LANES), F32),
             pltpu.VMEM((8, 2 * BASIS, SLOTS, NEAR), F32),
             pltpu.VMEM((8, 4, SLOTS, NEAR), F32),
-            pltpu.VMEM((8, 8, NEAR), F32),
+            pltpu.VMEM((8, TILE, NEAR), F32),
             pltpu.VMEM((3, LANES, LANES), F32),
-            pltpu.VMEM((27, 8, LANES), F32),
+            pltpu.VMEM((27, TILE, LANES), F32),
             *[pltpu.VMEM((ROWS, 2 * LANES), BF16)] * STEP,
             *[pltpu.VMEM((ROWS, 2 * GHOST), BF16)] * STEP,
             *[pltpu.VMEM((ROWS, 256), F32)] * STEP,

time: 48.5 us -> 46.9 us (0.967)
  Pallas kernels: 45.8 us -> 44.2 us
    pallas_call x1, Pallas kernels: 45.8 us -> 44.2 us  [per_device(): pl.pallas_call(whole_kernel, out_shape=(jax.ShapeDtypeStruct((2, 2, 2, SL...]
where the time goes in v5:
time: 46.9 us; the launch traced here: 46.7 us
  Pallas kernels  44.2 us (94%)
  local copies, waits for them, and re-layouts  1.88 us (4%)
  between operations  0.65 us (1%)
    pallas_call x1, Pallas kernels, per_device(): pl.pallas_call(whole_kernel, out_shape=(jax.ShapeDtypeStruct((2, 2, 2, SL...  44.2 us
    unnamed x4, local copies, waits for them, and re-layouts  1.88 us

profile of v5, /device:TPU:1, one launch (start us, length us, event | category | flops | bytes accessed | tf_op | source)
XLA Modules:
  0.0 46.7 jit_solution(4733680830298823223)
XLA Ops:
  0.6 44.2 %shard_map.95 = (f32[2,2,2,16]{3,2,1,0:T(2,128)}, f32[2,2,3,2,16]{4,3,2,1,0:T(2,128)}) custom-call(f32[2,2,3,2,16]{4,3,2,1,0:T(2,128)} %bitcast.3, f32[2,2,2,16,128]{4,3,2,1,0:T(8,128)} %feat_hbm.1, s32[2,2,2,16]{3,2,1,0:T(2,128)} %species_hbm.1, s32[2,2,2]{2,1,0:T(2,128)} %counts_hbm.1, f32[10]{0:T(128)} %table_hbm.1, f32[3,8,128]{2,1,0:T(8,128)} %bitcast.4, ...), custom_call_target="tpu_custom_call" | custom-call | tf_op jit(solution)/shard_map/pallas_call | solution.py:539
  44.8 0.0 copy-start
  44.9 1.3 %copy.12 = f32[2,2,2,16]{3,2,1,0:T(2,128)} copy(f32[2,2,2,16]{3,2,1,0:T(2,128)} %get-tuple-element.8) | data formatting | bytes 1024
  46.1 0.0 copy-done
  46.1 0.6 %copy.13 = f32[2,2,2,3,16]{4,2,3,1,0:T(2,128)} copy(f32[2,2,2,3,16]{4,2,3,1,0:T(2,128)S(1)} %bitcast.5) | data formatting | bytes 3072
Async XLA Ops:
  44.8 1.3 %copy-start = (f32[2,2,3,2,16]{4,3,2,1,0:T(2,128)S(1)}, f32[2,2,3,2,16]{4,3,2,1,0:T(2,128)}, u32[]{:S(2)}) copy-start(f32[2,2,3,2,16]{4,3,2,1,0:T(2,128)} %get-tuple-element.5) | copy-start | bytes 4612

commit v6 on v5

--- a/solution.py
+++ b/solution.py
@@ -348,7 +348,6 @@
     opair, pair, mom, gpair, odpair, dpair = (
         buffers[i * STEP : (i + 1) * STEP] for i in range(6)
     )
-    barrier = greet()
     held = [
         pltpu.make_async_copy(source, target, loads.at[i])
         for i, (source, target) in enumerate(
@@ -358,7 +357,10 @@
             )
         )
     ]
-    for copy in held:
+    for copy in held[:3]:
+        copy.start()
+    barrier = greet()
+    for copy in held[3:]:
         copy.start()
     slot = lax.broadcasted_iota(jnp.int32, (SLOTS, LANES), 0)
     tiles[SELF] = jnp.zeros((TILE, LANES), F32)

time: 46.9 us -> 46.9 us (level)
  no operation moved by 1% of the time
where the time goes in v6:
time: 46.9 us; the launch traced here: 46.7 us
  Pallas kernels  44.2 us (94%)
  local copies, waits for them, and re-layouts  1.88 us (4%)
  between operations  0.65 us (1%)
    pallas_call x1, Pallas kernels, per_device(): pl.pallas_call(whole_kernel, out_shape=(jax.ShapeDtypeStruct((2, 2, 2, SL...  44.2 us
    unnamed x4, local copies, waits for them, and re-layouts  1.88 us

profile of v6, /device:TPU:1, one launch (start us, length us, event | category | flops | bytes accessed | tf_op | source)
XLA Modules:
  0.0 46.7 jit_solution(16673301568025033986)
XLA Ops:
  0.6 44.2 %shard_map.95 = (f32[2,2,2,16]{3,2,1,0:T(2,128)}, f32[2,2,3,2,16]{4,3,2,1,0:T(2,128)}) custom-call(f32[2,2,3,2,16]{4,3,2,1,0:T(2,128)} %bitcast.3, f32[2,2,2,16,128]{4,3,2,1,0:T(8,128)} %feat_hbm.1, s32[2,2,2,16]{3,2,1,0:T(2,128)} %species_hbm.1, s32[2,2,2]{2,1,0:T(2,128)} %counts_hbm.1, f32[10]{0:T(128)} %table_hbm.1, f32[3,8,128]{2,1,0:T(8,128)} %bitcast.4, ...), custom_call_target="tpu_custom_call" | custom-call | tf_op jit(solution)/shard_map/pallas_call | solution.py:541
  44.8 0.0 copy-start
  44.9 1.3 %copy.12 = f32[2,2,2,16]{3,2,1,0:T(2,128)} copy(f32[2,2,2,16]{3,2,1,0:T(2,128)} %get-tuple-element.8) | data formatting | bytes 1024
  46.1 0.0 copy-done
  46.1 0.6 %copy.13 = f32[2,2,2,3,16]{4,2,3,1,0:T(2,128)} copy(f32[2,2,2,3,16]{4,2,3,1,0:T(2,128)S(1)} %bitcast.5) | data formatting | bytes 3072
Async XLA Ops:
  44.8 1.3 %copy-start = (f32[2,2,3,2,16]{4,3,2,1,0:T(2,128)S(1)}, f32[2,2,3,2,16]{4,3,2,1,0:T(2,128)}, u32[]{:S(2)}) copy-start(f32[2,2,3,2,16]{4,3,2,1,0:T(2,128)} %get-tuple-element.5) | copy-start | bytes 4612
